TPU v7x, 32 devices: a whole 2x2x4 slice. The times are simulated.
32 devices in a mesh: groups: 2 (over x), mesh: 16 (over z, y, core).
Axes of the slice: x: 2, y: 2, z: 4, core: 2. Of those that a mesh axis runs over, the one named last changes fastest.
Arguments:
- mesh_state: bfloat16 [128, 128, 512], P(('groups', 'mesh')), parts along dimension 0, may hold values from -8 to 8
- obs_latent: bfloat16 [1024, 128, 512], P(('groups', 'mesh')), parts along dimension 0, may hold values from -6 to 6
- pair_coupling: bfloat16 [1024, 128, 128], P(('groups', 'mesh')), parts along dimension 0, may hold values from -0.5 to 0.5
- pair_target: int32 [1024], P(('groups', 'mesh')), parts along dimension 0, may hold values from 0 to 11
- pair_source: int32 [1024], P(('groups', 'mesh')), parts along dimension 0, may hold values from 0 to 31
- pair_count: int32 [32], P(('groups', 'mesh')), parts along dimension 0, may hold values from 1 to 32, 256 in all
- mesh_coupling: bfloat16 [64, 4, 128, 128], P('mesh'), may hold values from -0.25 to 0.25
- neighbor: int32 [64, 4], P('mesh'), may hold values from 0 to 5, as said below
- rim_send: int32 [16, 2], P('mesh'), may hold values from 0 to 3, as said below
- enc_gain: float32 [512], replicated, may hold values from 0.25 to 1.75
- enc_self: bfloat16 [512, 512], replicated, may hold values from -0.25 to 0.25
- enc_obs: bfloat16 [512, 512], replicated, may hold values from -0.25 to 0.25
- enc_out: bfloat16 [512, 512], replicated, may hold values from -0.25 to 0.25
- node_gain: float32 [2, 512], replicated, may hold values from 0.25 to 1.75
- node_self: bfloat16 [2, 512, 512], replicated, may hold values from -0.25 to 0.25
- node_msg: bfloat16 [2, 512, 512], replicated, may hold values from -0.25 to 0.25
- node_out: bfloat16 [2, 512, 512], replicated, may hold values from -0.25 to 0.25
Outputs:
- mesh_out: bfloat16 [128, 128, 512], P(('groups', 'mesh')), parts along dimension 0
There are 2 independent parts, one for each index of `groups`. A program takes and returns all parts, laid end to end along the dimension named above; an argument that names none is the same for every part. Nothing has to cross between parts.
Inputs may be any that keep to these rules, and one draw needn't show every extreme that they name: pair_target // 4 - 1 is the offset (-1, 0 or 1) along mesh, modulo 16, from the pair's device to the device that owns the fed block; pair_target mod 4 is that block's local index there. `pair_source`: local observation block on the pair's own device. A device's live pairs are its first pair_count slots; some device has all 32 live. `neighbor`: values index a device's receive list: 0 the block from the left neighbour, 1 + c the local block c, 5 the block from the right neighbour; the entry at position 0 of each row is the block itself, the entry at position 1 lies before it in this list, the entry at position 2 after it. `rim_send`: two different local blocks of each device: the one sent to the left neighbour, then the one sent to the right.
All inputs are finite; a program needn't handle non-finite values.
Results may differ from a plain program's by a relative error of at most 0.014.
Values may be sent and summed in bfloat16 or wider, within the bound.
No kernel may reach another device: no remote copies, remote signals or barrier semaphores. Data moves between devices by JAX's collectives and lax.ppermute only.
A program may use at most 128 MiB of HBM per device.

v0:
```python
import jax
import jax.numpy as jnp
from jax import lax
from jax.sharding import PartitionSpec as P


def padded(cells, sides, width):
    for axis, dim in sides:
        count = lax.axis_size(axis)
        head = lax.slice_in_dim(cells, 0, width, axis=dim)
        tail = lax.slice_in_dim(cells, cells.shape[dim] - width, cells.shape[dim], axis=dim)
        cells = jnp.concatenate(
            [
                lax.ppermute(tail, axis, [(i, (i + 1) % count) for i in range(count)]),
                cells,
                lax.ppermute(head, axis, [((i + 1) % count, i) for i in range(count)]),
            ],
            axis=dim,
        )
    return cells


def from_behind(block, axis, distance):
    devices = range(lax.axis_size(axis))
    route = [((i - distance) % len(devices), i) for i in devices]
    return lax.ppermute(block, axis, route)


def layer_norm(values, scale_row):
    values = values.astype(jnp.float32)
    center = values - jnp.mean(values, axis=-1, keepdims=True)
    spread = jnp.mean(center * center, axis=-1, keepdims=True)
    return center * lax.rsqrt(spread + 1e-05) * scale_row


def node_update(current, normed, incoming, w_first, w_second, w_last):
    feature_width = current.shape[2]
    flat_norm = normed.reshape(-1, feature_width)
    flat_in = incoming.reshape(-1, feature_width)
    before = jnp.dot(flat_norm, w_first, preferred_element_type=jnp.float32)
    before = before + jnp.dot(flat_in, w_second, preferred_element_type=jnp.float32)
    hidden = jax.nn.silu(before).astype(jnp.bfloat16)
    updated = current.reshape(-1, feature_width).astype(jnp.float32) + jnp.dot(
        hidden, w_last, preferred_element_type=jnp.float32
    )
    return updated.astype(jnp.bfloat16).reshape(current.shape)


def pair_sums(coupling, chosen, weights):
    products = jnp.einsum("nij,njd->nid", coupling, chosen, preferred_element_type=jnp.float32)
    return jnp.einsum(
        "tn,nid->tid",
        weights,
        products,
        preferred_element_type=jnp.float32,
        precision=lax.Precision.HIGHEST,
    )


def shards(
    mesh_state,
    obs_latent,
    pair_coupling,
    pair_target,
    pair_source,
    pair_count,
    mesh_coupling,
    neighbor,
    rim_send,
    enc_gain,
    enc_self,
    enc_obs,
    enc_out,
    node_gain,
    node_self,
    node_msg,
    node_out,
):
    local_blocks = mesh_state.shape[0]
    pair_slots = pair_target.shape[0]
    slot_index = jnp.arange(pair_slots, dtype=jnp.int32)
    obs_total = obs_latent.size
    coupling_total = pair_coupling.size
    record = jnp.concatenate(
        [
            obs_latent.reshape(-1),
            pair_coupling.reshape(-1),
            pair_target.astype(jnp.bfloat16),
            pair_source.astype(jnp.bfloat16),
            pair_count.astype(jnp.bfloat16),
        ]
    )[None, :]
    received = padded(record, (("mesh", 0),), 1)
    window_latent = received[:, :obs_total].reshape((3,) + obs_latent.shape)
    window_coupling = received[:, obs_total : obs_total + coupling_total].reshape(
        (3 * pair_slots,) + pair_coupling.shape[1:]
    )
    integers = received[:, obs_total + coupling_total :].astype(jnp.int32)
    targets = integers[:, :pair_slots]
    sources = integers[:, pair_slots : 2 * pair_slots]
    counts = integers[:, 2 * pair_slots]
    neighbor_row = jnp.arange(3, dtype=jnp.int32)[:, None]
    alive = (slot_index[None, :] < counts[:, None]) & (targets // local_blocks == 2 - neighbor_row)
    block_ids = jnp.arange(local_blocks, dtype=jnp.int32)
    weights = (
        ((targets % local_blocks).reshape(-1)[None, :] == block_ids[:, None])
        & alive.reshape(-1)[None, :]
    ).astype(jnp.float32)
    chosen = window_latent[neighbor_row, sources].reshape((3 * pair_slots,) + obs_latent.shape[1:])
    enc_sum = pair_sums(window_coupling, chosen, weights)
    enc_in = enc_sum.astype(jnp.bfloat16)
    normed = layer_norm(mesh_state, enc_gain).astype(jnp.bfloat16)
    current = node_update(mesh_state, normed, enc_in, enc_self, enc_obs, enc_out)
    for round_index in range(node_gain.shape[0]):
        normed = layer_norm(current, node_gain[round_index]).astype(jnp.bfloat16)
        to_left = normed[rim_send[0, 0]]
        to_right = normed[rim_send[0, 1]]
        from_left = from_behind(to_right, "mesh", 1)
        from_right = from_behind(to_left, "mesh", -1)
        extended = jnp.concatenate([from_left[None], normed, from_right[None]], axis=0)
        gathered = extended[neighbor]
        message = jnp.einsum(
            "bkij,bkjd->bid", mesh_coupling, gathered, preferred_element_type=jnp.float32
        ).astype(jnp.bfloat16)
        current = node_update(
            current,
            normed,
            message,
            node_self[round_index],
            node_msg[round_index],
            node_out[round_index],
        )
    return current


def solution(mesh):
    return jax.shard_map(
        shards,
        mesh=mesh,
        in_specs=(
            P(("groups", "mesh"), None, None),
            P(("groups", "mesh"), None, None),
            P(("groups", "mesh"), None, None),
            P(("groups", "mesh")),
            P(("groups", "mesh")),
            P(("groups", "mesh")),
            P("mesh", None, None, None),
            P("mesh", None),
            P("mesh", None),
            P(),
            P(),
            P(),
            P(),
            P(),
            P(),
            P(),
            P(),
        ),
        out_specs=P(("groups", "mesh"), None, None),
        check_vma=False,
    )
```

profile of v0, /device:TPU:1, one launch (start us, length us, event | category | flops | bytes accessed | tf_op | source)
XLA Modules:
  0.0 491.3 jit_solution(7027650898708833474)
XLA Ops:
  0.7 0.7 convert_element_type.98
  1.4 0.7 convert_element_type.99
  2.0 6.3 %copy.22 = bf16[512,4,8,128]{3,1,2,0:T(4,128)(2,1)} copy(bf16[512,4,8,128]{3,2,1,0:T(8,128)(2,1)} %bitcast.109) | data formatting | bytes 8388608
  8.3 76.5 %concatenate.15 = bf16[2621505]{0:T(1024)(128)(2,1)} concatenate(bf16[2097152]{0:T(1024)(128)(2,1)} %bitcast.103, bf16[524288]{0:T(1024)(128)(2,1)} %bitcast.113, bf16[32]{0:T(256)(128)(2,1)S(1)} %convert_element_type.98, bf16[32]{0:T(256)(128)(2,1)S(1)} %convert_element_type.99, bf16[1]{0:T(256)(128)(2,1)S(6)} %convert_element_type.100), dimensions={0} | concatenate | bytes 10486020 | tf_op jit(solution)/shard_map/concatenate | solution.py:84
  84.8 8.1 %broadcast_in_dim.16 = bf16[1,2621505]{1,0:T(2,128)(2,1)} reshape(bf16[2621505]{0:T(1024)(128)(2,1)} %concatenate.15) | data formatting | bytes 10486020 | tf_op jit(solution)/shard_map/broadcast_in_dim | solution.py:84
  93.0 2.8 collective-permute-start
  100.4 0.6 pad_clamp_fusion
  101.8 1.4 fusion.64
  103.2 218.6 %collective-permute-done.1 = bf16[1,2621505]{1,0:T(2,128)(2,1)} collective-permute-done((bf16[1,2621505]{1,0:T(2,128)(2,1)}, bf16[1,2621505]{1,0:T(2,128)(2,1)}, u32[]{:S(2)}, u32[]{:S(2)}) %collective-permute-start.1) | collective-permute-done | bytes 5243042 | tf_op jit(solution)/shard_map/ppermute | solution.py:16
  321.9 0.7 maximum_convert_fusion
  322.9 0.6 and.26
  323.6 0.6 eq.25
  324.2 12.7 %pad_maximum_fusion.2 = bf16[3,524288]{1,0:T(4,128)(2,1)} fusion(bf16[1,2621505]{1,0:T(2,128)(2,1)} %collective-permute-done.1, bf16[1,2621505]{1,0:T(2,128)(2,1)} %broadcast_in_dim.16, bf16[1,2621505]{1,0:T(2,128)(2,1)} %collective-permute-done), kind=kLoop, calls=%fused_computation.7 | loop fusion | flops 9437184 | bytes 18874758 | tf_op jit(solution)/shard_map/slice | solution.py:95
  336.9 7.9 %reshape.134 = bf16[96,128,128]{2,1,0:T(8,128)(2,1)} reshape(bf16[3,524288]{1,0:T(4,128)(2,1)} %pad_maximum_fusion.2) | data formatting | bytes 6291456 | tf_op jit(solution)/shard_map/reshape | solution.py:95
  344.8 53.6 %pad_maximum_fusion = bf16[3,2097152]{1,0:T(4,128)(2,1)S(1)} fusion(bf16[1,2621505]{1,0:T(2,128)(2,1)} %collective-permute-done.1, bf16[1,2621505]{1,0:T(2,128)(2,1)} %broadcast_in_dim.16, bf16[1,2621505]{1,0:T(2,128)(2,1)} %collective-permute-done), kind=kLoop, calls=%fused_computation.5 | loop fusion | flops 37748736 | bytes 28311942 | tf_op jit(solution)/shard_map/concatenate | solution.py:12
  398.4 10.8 %copy.23 = bf16[1,3,4096,512]{3,2,1,0:T(8,128)(2,1)} copy(bf16[1,3,4096,512]{3,1,2,0:T(4,128)(2,1)S(1)} %bitcast.101) | data formatting | bytes 25165824
  409.2 11.8 %gather_fusion = bf16[96,128,512]{2,1,0:T(8,128)(2,1)} fusion(bf16[3,32,128,512]{3,2,1,0:T(8,128)(2,1)} %bitcast.102, s32[96]{0:T(128)S(1)} %reshape.144), kind=kCustom, calls=%fused_computation | custom fusion | bytes 25166592 | tf_op jit(solution)/shard_map/gather | solution.py:109
  421.0 17.3 %fusion.65 = f32[96,128,512]{2,1,0:T(8,128)} fusion(bf16[96,128,128]{2,1,0:T(8,128)(2,1)} %reshape.134, bf16[96,128,512]{2,1,0:T(8,128)(2,1)} %gather_fusion), kind=kOutput, calls=%fused_computation.110 | convolution fusion | flops 1610612736 | bytes 40894464 | tf_op jit(solution)/shard_map/nij,njd->nid/dot_general | solution.py:50
  438.3 27.7 %fusion.2 = bf16[4,128,512]{2,0,1:T(4,128)(2,1)S(1)} fusion(f32[96,128,512]{2,1,0:T(8,128)} %fusion.65, s32[96]{0:T(128)S(1)} %copy-done.8, pred[96]{0:T(512)(128)(4,1)S(1)} %copy-done.12), kind=kOutput, calls=%fused_computation.16 | convolution fusion | flops 302252800 | bytes 25690592 | tf_op jit(solution)/shard_map/tn,nid->tid/dot_general | solution.py:51
  466.0 0.9 copy.18
  466.9 2.3 fusion.60
  469.8 2.0 collective-permute-start.2
  471.8 2.6 fusion.12
  474.9 1.3 collective-permute-done.3
  476.3 0.8 gather_fusion.1
  477.6 2.8 fusion.61
  480.9 1.2 collective-permute-start.4
  482.1 2.6 fusion.13
  484.7 0.8 collective-permute-done.4
  485.4 1.1 collective-permute-done.5
  486.6 0.7 gather_fusion.2
  487.8 3.5 fusion.11
  (60 shorter events, 4.6 us)
Async XLA Ops:
  0.0 477.1 %copy-start = (bf16[4,4,128,128]{3,2,1,0:T(8,128)(2,1)S(1)}, bf16[4,4,128,128]{3,2,1,0:T(8,128)(2,1)}, u32[]{:S(2)}) copy-start(bf16[4,4,128,128]{3,2,1,0:T(8,128)(2,1)} %param.23) | copy-start | bytes 1572868
  84.8 11.1 %copy-start.11 = (s32[1,2]{1,0:T(1,128)S(1)}, s32[1,2]{1,0:T(1,128)}, u32[]{:S(2)}) copy-start(s32[1,2]{1,0:T(1,128)} %param.25) | copy-start | bytes 28
  84.8 14.2 %copy-start.10 = (s32[4,4]{1,0:T(4,128)S(1)}, s32[4,4]{1,0:T(4,128)}, u32[]{:S(2)}) copy-start(s32[4,4]{1,0:T(4,128)} %param.24) | copy-start | bytes 196
  84.8 16.2 %copy-start.3 = (bf16[4,128,512]{2,1,0:T(8,128)(2,1)S(1)}, bf16[4,128,512]{2,1,0:T(8,128)(2,1)}, u32[]{:S(2)}) copy-start(bf16[4,128,512]{2,1,0:T(8,128)(2,1)} %param.17) | copy-start | bytes 1572868
  84.8 16.7 %copy-start.7 = (f32[2,512]{1,0:T(2,128)S(1)}, f32[2,512]{1,0:T(2,128)}, u32[]{:S(2)}) copy-start(f32[2,512]{1,0:T(2,128)} %param.30) | copy-start | bytes 12292
  84.8 16.7 %copy-start.9 = (f32[512]{0:T(512)S(1)}, f32[512]{0:T(512)}, u32[]{:S(2)}) copy-start(f32[512]{0:T(512)} %param.26) | copy-start | bytes 6148
  84.8 17.0 %copy-start.5 = (bf16[512,512]{1,0:T(8,128)(2,1)S(1)}, bf16[512,512]{1,0:T(8,128)(2,1)}, u32[]{:S(2)}) copy-start(bf16[512,512]{1,0:T(8,128)(2,1)} %param.27) | copy-start | bytes 1572868
  93.0 228.9 %collective-permute-start.1 = (bf16[1,2621505]{1,0:T(2,128)(2,1)}, bf16[1,2621505]{1,0:T(2,128)(2,1)}, u32[]{:S(2)}, u32[]{:S(2)}) collective-permute-start(bf16[1,2621505]{1,0:T(2,128)(2,1)} %broadcast_in_dim.16), channel_id=1, source_target_pairs={{1,0},{2,1},{3,2},{4,3},{5,4},{6,5},{7,6},{8,7},{9,8},{10,9},{11,1... | collective-permute-start | bytes 15729038 | tf_op jit(solution)/shard_map/ppermute | solution.py:16
  93.0 228.9 %collective-permute-start = (bf16[1,2621505]{1,0:T(2,128)(2,1)}, bf16[1,2621505]{1,0:T(2,128)(2,1)}, u32[]{:S(2)}, u32[]{:S(2)}) collective-permute-start(bf16[1,2621505]{1,0:T(2,128)(2,1)} %broadcast_in_dim.16), channel_id=1, source_target_pairs={{0,1},{1,2},{2,3},{3,4},{4,5},{5,6},{6,7},{7,8},{8,9},{9,10},{10,1... | collective-permute-start | bytes 15729038 | tf_op jit(solution)/shard_map/ppermute | solution.py:14
  421.0 17.3 %copy-start.8 = (s32[96]{0:T(128)S(1)}, s32[96]{0:T(128)}, u32[]{:S(2)}) copy-start(s32[96]{0:T(128)} %eq.25) | copy-start | bytes 1156
  421.0 17.3 %copy-start.12 = (pred[96]{0:T(512)(128)(4,1)S(1)}, pred[96]{0:T(512)(128)(4,1)}, u32[]{:S(2)}) copy-start(pred[96]{0:T(512)(128)(4,1)} %and.26) | copy-start | bytes 292
  438.3 28.6 %copy-start.4 = (f32[512,512]{1,0:T(8,128)S(1)}, f32[512,512]{1,0:T(8,128)}, u32[]{:S(2)}) copy-start(f32[512,512]{1,0:T(8,128)} %fusion.64) | copy-start | bytes 3145732
  469.2 7.0 %copy-start.2 = (f32[512,512]{1,0:T(8,128)}, f32[512,512]{1,0:T(8,128)S(1)}, u32[]{:S(2)}) copy-start(f32[512,512]{1,0:T(8,128)S(1)} %get-tuple-element.24) | copy-start | bytes 3145732
  469.8 5.1 %collective-permute-start.2 = (bf16[128,512]{1,0:T(8,128)(2,1)S(1)}, bf16[128,512]{1,0:T(8,128)(2,1)S(1)}, u32[]{:S(2)}, u32[]{:S(2)}) collective-permute-start(bf16[128,512]{1,0:T(8,128)(2,1)S(1)} %get-tuple-element.9), channel_id=1, source_target_pairs={{15,0},{0,1},{1,2},{2,3},{3,4},{4,5},{5,6},{6,7},{7,8},{8,9},{9,10... | collective-permute-start | bytes 393224 | tf_op jit(solution)/shard_map/ppermute | solution.py:26
  471.8 4.4 collective-permute-start.3
  477.1 9.5 %copy-start.6 = (s32[1024]{0:T(1024)S(1)}, s32[1024]{0:T(1024)}, u32[]{:S(2)}) copy-start(s32[1024]{0:T(1024)} %pad_clamp_fusion) | copy-start | bytes 12292
  480.4 6.1 %copy-start.1 = (f32[512,512]{1,0:T(8,128)}, f32[512,512]{1,0:T(8,128)S(1)}, u32[]{:S(2)}) copy-start(f32[512,512]{1,0:T(8,128)S(1)} %get-tuple-element.26) | copy-start | bytes 3145732
  480.9 4.5 collective-permute-start.4
  482.1 4.4 collective-permute-start.5
where the time goes:
time: 500 us; the launch traced here: 491 us
  waiting for transfers between devices  222 us (44%)
  local copies, waits for them, and re-layouts  126 us (25%)
  other arithmetic  70.9 us (14%)
  matrix products  61 us (12%)
  starting transfers between devices  6.09 us (1%)
    ppermute x1, waiting for transfers between devices, padded(): lax.ppermute(head, axis, [((i + 1) % count, i) for i in range(count)])  219 us
    concatenate x1, local copies, waits for them, and re-layouts, shards(): jnp.concatenate([obs_latent.reshape(-1), pair_coupling.reshape(-1), pair_...  76.5 us
    concatenate x1, other arithmetic, padded(): jnp.concatenate([lax.ppermute(tail, axis, [(i, (i + 1) % count) for i in...  53.6 us
    dot_general x1, matrix products, pair_sums(): jnp.einsum('tn,nid->tid', weights, products, preferred_element_type=jnp.f...  27.7 us
    dot_general x1, matrix products, pair_sums(): jnp.einsum('nij,njd->nid', coupling, chosen, preferred_element_type=jnp.f...  17.3 us
    unnamed x28, local copies, waits for them, and re-layouts  17.2 us
    slice x1, other arithmetic, shards(): received[:, obs_total:obs_total + coupling_total]  12.7 us
    gather x1, local copies, waits for them, and re-layouts, shards(): window_latent[neighbor_row, sources]  11.8 us
  transfers between devices with their start and end apart: 6, of which 5 were waited for; matrix products, arithmetic and copies ran while one was open for 2% of the time, Pallas kernels for 0%

commit v1 on v0

v1 whole, which is shorter than its diff:
```python
import jax
import jax.numpy as jnp
from jax import lax
from jax.experimental import pallas as pl
from jax.experimental.pallas import tpu as pltpu
from jax.sharding import PartitionSpec as P

F32 = jnp.float32
BF16 = jnp.bfloat16
VMEM = pl.BlockSpec(memory_space=pltpu.VMEM)
SMEM = pl.BlockSpec(memory_space=pltpu.SMEM)
ANY = pl.BlockSpec(memory_space=pl.ANY)


def dot(a, b):
    return jnp.dot(a, b, preferred_element_type=F32)


def silu(v):
    half = 0.5 * v
    return half + half * jnp.tanh(half)


def norm_rows(values, gain):
    center = values - jnp.mean(values, axis=-1, keepdims=True)
    spread = jnp.mean(center * center, axis=-1, keepdims=True)
    return (center * lax.rsqrt(spread + 1e-05) * gain).astype(BF16)


def odd_device():
    return lax.rem(lax.axis_index("mesh"), 2)


def block_order(rim):
    odd = odd_device()
    off = rim[0, odd]
    on = rim[0, 1 - odd]
    low = jnp.minimum(off, on)
    high = jnp.maximum(off, on)
    third = jnp.where(low > 0, 0, jnp.where(high > 1, 1, 2))
    fourth = jnp.where(high < 3, 3, jnp.where(low < 2, 2, 1))
    return [off, on, third, fourth]


def pair_kernel(side, tgt, src, cnt, obs, cpl, out, xbuf, cbuf, acc, xsem, csem):
    blocks = out.shape[0]
    odd = odd_device()
    part = {"off": 2 * odd, "on": 2 - 2 * odd, "self": 1}[side]
    live = cnt[0]

    def local(e):
        t = tgt[e] - part * blocks
        return t, (t >= 0) & (t < blocks)

    def count(e, word):
        t, mine = local(e)
        return word + jnp.where(mine, 1 << (8 * jnp.clip(t, 0, blocks - 1)), 0)

    word = lax.fori_loop(0, live, count, jnp.int32(0))
    counts = [(word >> (8 * t)) & 255 for t in range(blocks)]
    firsts, place = [], jnp.int32(0)
    total = jnp.int32(0)
    for t in range(blocks):
        firsts.append(total)
        place = place + (total << (8 * t))
        total = total + counts[t]

    def fetch(e, place):
        t, mine = local(e)
        shift = 8 * jnp.clip(t, 0, blocks - 1)

        @pl.when(mine)
        def _():
            slot = (place >> shift) & 255
            pltpu.make_async_copy(obs.at[src[e]], xbuf.at[slot], xsem.at[slot]).start()
            pltpu.make_async_copy(cpl.at[e], cbuf.at[slot], csem.at[slot]).start()

        return place + jnp.where(mine, 1 << shift, 0)

    lax.fori_loop(0, live, fetch, place)

    def arrive(slot):
        pltpu.make_async_copy(obs.at[0], xbuf.at[slot], xsem.at[slot]).wait()
        pltpu.make_async_copy(cpl.at[0], cbuf.at[slot], csem.at[slot]).wait()

    for t in range(blocks):
        acc[...] = jnp.zeros_like(acc)

        def two(j, carry):
            slot = firsts[t] + 2 * j
            arrive(slot)
            arrive(slot + 1)
            left = jnp.concatenate([cbuf[slot], cbuf[slot + 1]], axis=1)
            right = jnp.concatenate([xbuf[slot], xbuf[slot + 1]], axis=0)
            acc[...] += dot(left, right)
            return carry

        lax.fori_loop(0, counts[t] // 2, two, 0)

        @pl.when(counts[t] % 2 == 1)
        def _():
            slot = firsts[t] + counts[t] - 1
            arrive(slot)
            acc[...] += dot(cbuf[slot], xbuf[slot])

        out[t] = acc[...].astype(out.dtype)


def pair_sums(side, dtype, blocks, tgt, src, cnt, obs, cpl):
    slots, rows, width = tgt.shape[0], obs.shape[1], obs.shape[2]
    return pl.pallas_call(
        lambda *refs: pair_kernel(side, *refs),
        out_shape=jax.ShapeDtypeStruct((blocks, rows, width), dtype),
        in_specs=[SMEM, SMEM, SMEM, ANY, ANY],
        out_specs=VMEM,
        scratch_shapes=[
            pltpu.VMEM((slots, rows, width), BF16),
            pltpu.VMEM((slots, rows, rows), BF16),
            pltpu.VMEM((rows, width), F32),
            pltpu.SemaphoreType.DMA((slots,)),
            pltpu.SemaphoreType.DMA((slots,)),
        ],
        compiler_params=pltpu.CompilerParams(vmem_limit_bytes=12 << 20),
        cost_estimate=pl.CostEstimate(flops=10 * 2 * 128 * 128 * 512, bytes_accessed=4 << 20, transcendentals=0),
        name="pairs_" + side,
    )(tgt, src, cnt, obs, cpl)


def call(kernel, out, *args, specs=None, flops=0, moved=1 << 20, name=None):
    return pl.pallas_call(
        kernel,
        out_shape=out,
        in_specs=specs or [VMEM] * len(args),
        out_specs=jax.tree.map(lambda _: VMEM, out),
        compiler_params=pltpu.CompilerParams(vmem_limit_bytes=14 << 20),
        cost_estimate=pl.CostEstimate(flops=flops, bytes_accessed=moved, transcendentals=0),
        name=name,
    )(*args)


def prepare_kernel(rim, nbr, state, gain, w_self, coupling, pre, state_p, mix):
    blocks, rows = state.shape[0], state.shape[1]
    order = block_order(rim)
    odd = odd_device()
    last = blocks + 1
    codes = [1 + o for o in order] + [last * odd, last - last * odd]
    for i, m in enumerate(order):
        cut = pl.ds(i * rows, rows)
        values = state[m]
        state_p[cut, :] = values
        pre[cut, :] = dot(norm_rows(values.astype(F32), gain[...]), w_self[...])
        for c, code in enumerate(codes):
            total = None
            for k in range(coupling.shape[1]):
                term = jnp.where(nbr[m, k] == code, coupling[m, k].astype(F32), 0.0)
                total = term if total is None else total + term
            mix[cut, c * rows : (c + 1) * rows] = total.astype(BF16)


def encode_kernel(rim, pre, state_p, own, on, off, w_obs, w_out, gain, state, normed):
    rows = own.shape[1]
    for i, m in enumerate(block_order(rim)):
        cut = pl.ds(i * rows, rows)
        summed = (own[m] + on[m].astype(F32) + off[m].astype(F32)).astype(BF16)
        hidden = silu(pre[cut, :] + dot(summed, w_obs[...])).astype(BF16)
        updated = (state_p[cut, :].astype(F32) + dot(hidden, w_out[...])).astype(BF16)
        state[cut, :] = updated
        normed[cut, :] = norm_rows(updated.astype(F32), gain[...])


def local_kernel(normed, w_self, mix, pre, message):
    size = normed.shape[0]
    pre[...] = dot(normed[...], w_self[...])
    message[...] = dot(mix[:, :size], normed[...])


def round_kernel(last, rim, pre, message, mix, off, on, state, w_msg, w_out, gain, *outs):
    size = state.shape[0]
    rows = off.shape[0]
    rims = jnp.concatenate([off[...], on[...]], axis=0)
    for i, m in enumerate(block_order(rim)):
        cut = pl.ds(i * rows, rows)
        incoming = (message[cut, :] + dot(mix[cut, size:], rims)).astype(BF16)
        hidden = silu(pre[cut, :] + dot(incoming, w_msg[...])).astype(BF16)
        updated = (state[cut, :].astype(F32) + dot(hidden, w_out[...])).astype(BF16)
        if last:
            outs[0][m] = updated
        else:
            outs[0][cut, :] = updated
            outs[1][cut, :] = norm_rows(updated.astype(F32), gain[...])


def shards(
    mesh_state,
    obs_latent,
    pair_coupling,
    pair_target,
    pair_source,
    pair_count,
    mesh_coupling,
    neighbor,
    rim_send,
    enc_gain,
    enc_self,
    enc_obs,
    enc_out,
    node_gain,
    node_self,
    node_msg,
    node_out,
):
    blocks, rows, width = mesh_state.shape
    size = blocks * rows
    count = lax.axis_size("mesh")
    on_route = [(i, i ^ 1) for i in range(count)]
    off_route = [(i, (i + 1) % count if i % 2 else (i - 1) % count) for i in range(count)]

    def swap_off(x):
        return lax.ppermute(x, "mesh", off_route)

    def swap_on(x):
        return lax.ppermute(x, "mesh", on_route)

    def shape(*dims, dtype=BF16):
        return jax.ShapeDtypeStruct(dims, dtype)

    square = 2 * size * width * width
    pairs = (pair_target, pair_source, pair_count, obs_latent, pair_coupling)
    sums_off = swap_off(pair_sums("off", BF16, blocks, *pairs))
    sums_on = swap_on(pair_sums("on", BF16, blocks, *pairs))
    sums_own = pair_sums("self", F32, blocks, *pairs)
    pre, state_p, mix = call(
        prepare_kernel,
        (shape(size, width, dtype=F32), shape(size, width), shape(size, size + 2 * rows)),
        rim_send,
        neighbor,
        mesh_state,
        enc_gain[None],
        enc_self,
        mesh_coupling,
        specs=[SMEM, SMEM] + [VMEM] * 4,
        flops=2 * square,
        name="prepare",
    )
    state, normed = call(
        encode_kernel,
        (shape(size, width), shape(size, width)),
        rim_send,
        pre,
        state_p,
        sums_own,
        sums_on,
        sums_off,
        enc_obs,
        enc_out,
        node_gain[:1],
        specs=[SMEM] + [VMEM] * 8,
        flops=2 * square,
        name="encode",
    )
    rounds = node_gain.shape[0]
    for r in range(rounds):
        last = r == rounds - 1
        off = swap_off(normed[:rows])
        on = swap_on(normed[rows : 2 * rows])
        pre, message = call(
            local_kernel,
            (shape(size, width, dtype=F32), shape(size, width, dtype=F32)),
            normed,
            node_self[r],
            mix,
            flops=2 * square,
            name="local_part",
        )
        outs = call(
            lambda *refs, last=last: round_kernel(last, *refs),
            (shape(blocks, rows, width),) if last else (shape(size, width), shape(size, width)),
            rim_send,
            pre,
            message,
            mix,
            off,
            on,
            state,
            node_msg[r],
            node_out[r],
            node_gain[(r + 1) % rounds][None],
            specs=[SMEM] + [VMEM] * 9,
            flops=3 * square,
            name="round_rest",
        )
        if not last:
            state, normed = outs
    return outs[0]


def solution(mesh):
    block = P(("groups", "mesh"), None, None)
    return jax.shard_map(
        shards,
        mesh=mesh,
        in_specs=(
            block,
            block,
            block,
            P(("groups", "mesh")),
            P(("groups", "mesh")),
            P(("groups", "mesh")),
            P("mesh", None, None, None),
            P("mesh", None),
            P("mesh", None),
        )
        + (P(),) * 8,
        out_specs=block,
        check_vma=False,
    )
```

time: 500 us -> 50.5 us (0.10)
  the two profiles are of different devices: /device:TPU:1 before, /device:TPU:0 now
where the time goes in v1:
time: 50.5 us; the launch traced here: 50 us
  Pallas kernels  27.4 us (54%)
  starting transfers between devices  10.7 us (21%)
  waiting for transfers between devices  5.92 us (12%)
  local copies, waits for them, and re-layouts  5.04 us (10%)
  between operations  0.94 us (2%)
    pallas_call x3, Pallas kernels, pair_sums(): pl.pallas_call(lambda *refs: pair_kernel(side, *refs), out_shape=jax.Shap...  16.4 us
    pallas_call x6, Pallas kernels, call(): pl.pallas_call(kernel, out_shape=out, in_specs=specs or [VMEM] * len(args...  11.1 us
    ppermute x3, starting transfers between devices, swap_off(): return lax.ppermute(x, 'mesh', off_route)  10.6 us
    ppermute x3, waiting for transfers between devices, swap_off(): return lax.ppermute(x, 'mesh', off_route)  5.91 us
    unnamed x32, local copies, waits for them, and re-layouts  4.79 us
  transfers between devices with their start and end apart: 6, of which 3 were waited for; matrix products, arithmetic and copies ran while one was open for 0% of the time, Pallas kernels for 29%

profile of v1, /device:TPU:0, one launch (start us, length us, event | category | flops | bytes accessed | tf_op | source)
XLA Modules:
  0.0 50.0 jit_solution(4159659718600654591)
XLA Ops:
  0.7 2.2 %copy-done = bf16[32,128,512]{2,1,0:T(8,128)(2,1)S(1)} copy-done((bf16[32,128,512]{2,1,0:T(8,128)(2,1)S(1)}, bf16[32,128,512]{2,1,0:T(8,128)(2,1)}, u32[]{:S(2)}) %copy-start) | copy-done | bytes 4194328
  2.8 1.2 %copy-done.1 = bf16[32,128,128]{2,1,0:T(8,128)(2,1)S(1)} copy-done((bf16[32,128,128]{2,1,0:T(8,128)(2,1)S(1)}, bf16[32,128,128]{2,1,0:T(8,128)(2,1)}, u32[]{:S(2)}) %copy-start.1) | copy-done | bytes 1048600
  4.1 0.7 %copy-done.4 = s32[32]{0:T(128)S(1)} copy-done((s32[32]{0:T(128)S(1)}, s32[32]{0:T(128)}, u32[]{:S(2)}) %copy-start.4) | copy-done | bytes 152
  4.7 0.7 %copy-done.5 = s32[32]{0:T(128)S(1)} copy-done((s32[32]{0:T(128)S(1)}, s32[32]{0:T(128)}, u32[]{:S(2)}) %copy-start.5) | copy-done | bytes 152
  5.4 5.1 %pairs_on.1 = bf16[4,128,512]{2,1,0:T(8,128)(2,1)S(1)} custom-call(s32[32]{0:T(128)S(1)} %copy-done.4, s32[32]{0:T(128)S(1)} %copy-done.5, s32[1]{0:T(128)S(6)} %copy.18.refs_2_, bf16[32,128,512]{2,1,0:T(8,128)(2,1)S(1)} %copy-done, bf16[32,128,128]{2,1,0:T(8,128)(2,1)S(1)} %copy-done.1), custom_call_target="tpu_custom_call" | custom-call | flops 167772160 | bytes 4194304 | tf_op jit(solution)/shard_map/pairs_on/pallas_call | solution.py:111
  10.5 0.1 collective-permute-start
  10.5 5.8 %pairs_off.1 = bf16[4,128,512]{2,1,0:T(8,128)(2,1)S(1)} custom-call(s32[32]{0:T(128)S(1)} %copy-done.4, s32[32]{0:T(128)S(1)} %copy-done.5, s32[1]{0:T(128)S(6)} %copy.18.refs_2_, bf16[32,128,512]{2,1,0:T(8,128)(2,1)S(1)} %copy-done, bf16[32,128,128]{2,1,0:T(8,128)(2,1)S(1)} %copy-done.1), custom_call_target="tpu_custom_call" | custom-call | flops 167772160 | bytes 4194304 | tf_op jit(solution)/shard_map/pairs_off/pallas_call | solution.py:111
  16.3 0.0 copy-start.6
  16.3 0.0 copy-start.7
  16.3 0.0 copy-start.8
  16.3 0.0 copy-start.9
  16.4 0.0 copy-start.10
  16.4 0.0 copy-start.11
  16.4 0.0 copy-start.15
  16.4 0.0 copy-start.14
  16.4 3.5 %collective-permute-start.1 = (bf16[4,128,512]{2,1,0:T(8,128)(2,1)S(1)}, bf16[4,128,512]{2,1,0:T(8,128)(2,1)S(1)}, u32[]{:S(2)}, u32[]{:S(2)}) collective-permute-start(bf16[4,128,512]{2,1,0:T(8,128)(2,1)S(1)} %pairs_off.1), channel_id=1, source_target_pairs={{0,15},{1,2},{2,1},{3,4},{4,3},{5,6},{6,5},{7,8},{8,7},{9,10},{10,... | collective-permute-start | bytes 1572872 | tf_op jit(solution)/shard_map/ppermute | solution.py:219
  19.9 5.5 %pairs_self.1.own = f32[4,128,512]{2,1,0:T(8,128)S(1)} custom-call(s32[32]{0:T(128)S(1)} %copy-done.4, s32[32]{0:T(128)S(1)} %copy-done.5, s32[1]{0:T(128)S(6)} %copy.18.refs_2_, bf16[32,128,512]{2,1,0:T(8,128)(2,1)S(1)} %copy-done, bf16[32,128,128]{2,1,0:T(8,128)(2,1)S(1)} %copy-done.1), custom_call_target="tpu_custom_call" | custom-call | flops 167772160 | bytes 4194304 | tf_op jit(solution)/shard_map/pairs_self/pallas_call | solution.py:111
  25.5 0.0 copy-start.2
  25.5 0.0 copy-start.3
  25.6 1.9 %prepare.1 = (f32[512,512]{1,0:T(8,128)S(1)}, bf16[512,512]{1,0:T(8,128)(2,1)S(1)}, bf16[512,768]{1,0:T(8,128)(2,1)S(1)}) custom-call(s32[1,2]{1,0:T(1,128)S(1)} %copy-done.6, s32[4,4]{1,0:T(4,128)S(1)} %copy-done.10, bf16[4,128,512]{2,1,0:T(8,128)(2,1)S(1)} %copy-done.7, f32[1,512]{1,0:T(1,128)S(1)} %bitcast.13, bf16[512,512]{1,0:T(8,128)(2,1)S(1)} %copy-done.8, ...), custom_call_target="tpu_custom_call" | custom-call | flops 536870912 | bytes 1048576 | tf_op jit(solution)/shard_map/prepare/pallas_call | solution.py:130
  27.5 0.1 slice_bitcast_fusion
  27.7 0.2 collective-permute-done.1.off
  27.9 2.0 %encode.1 = (bf16[512,512]{1,0:T(8,128)(2,1)S(1)}, bf16[512,512]{1,0:T(8,128)(2,1)S(1)}) custom-call(s32[1,2]{1,0:T(1,128)S(1)} %copy-done.6, f32[512,512]{1,0:T(8,128)S(1)} %get-tuple-element.16.pre, bf16[512,512]{1,0:T(8,128)(2,1)S(1)} %get-tuple-element.17.state_p, f32[4,128,512]{2,1,0:T(8,128)S(1)} %pairs_self.1.own, ...), custom_call_target="tpu_custom_call" | custom-call | flops 536870912 | bytes 1048576 | tf_op jit(solution)/shard_map/encode/pallas_call | solution.py:130
  30.0 3.5 %collective-permute-start.2 = (bf16[128,512]{1,0:T(8,128)(2,1)S(1)}, bf16[128,512]{1,0:T(8,128)(2,1)S(1)}, u32[]{:S(2)}, u32[]{:S(2)}) collective-permute-start(bf16[128,512]{1,0:T(8,128)(2,1)S(1)} %get-tuple-element.36), channel_id=1, source_target_pairs={{0,15},{1,2},{2,1},{3,4},{4,3},{5,6},{6,5},{7,8},{8,7},{9,10},{10,... | collective-permute-start | bytes 393224 | tf_op jit(solution)/shard_map/ppermute | solution.py:219
  33.5 0.1 slice_bitcast_fusion.2
  33.6 0.7 %local_part.2 = (f32[512,512]{1,0:T(8,128)S(1)}, f32[512,512]{1,0:T(8,128)S(1)}) custom-call(bf16[512,512]{1,0:T(8,128)(2,1)S(1)} %get-tuple-element.18.normed, bf16[512,512]{1,0:T(8,128)(2,1)S(1)} %get-tuple-element.32.w_self, bf16[512,768]{1,0:T(8,128)(2,1)S(1)} %get-tuple-element.19.mix.refs_3_), custom_call_target="tpu_custom_call" | custom-call | flops 536870912 | bytes 1048576 | tf_op jit(solution)/shard_map/local_part/pallas_call | solution.py:130
  34.3 2.9 %collective-permute-done.2.refs_4_ = bf16[128,512]{1,0:T(8,128)(2,1)S(1)} collective-permute-done((bf16[128,512]{1,0:T(8,128)(2,1)S(1)}, bf16[128,512]{1,0:T(8,128)(2,1)S(1)}, u32[]{:S(2)}, u32[]{:S(2)}) %collective-permute-start.2) | collective-permute-done | bytes 131104 | tf_op jit(solution)/shard_map/ppermute | solution.py:219
  37.1 2.6 %round_rest.2 = (bf16[512,512]{1,0:T(8,128)(2,1)S(1)}, bf16[512,512]{1,0:T(8,128)(2,1)S(1)}) custom-call(s32[1,2]{1,0:T(1,128)S(1)} %copy-done.6, f32[512,512]{1,0:T(8,128)S(1)} %get-tuple-element.20.refs_1_, f32[512,512]{1,0:T(8,128)S(1)} %get-tuple-element.21.refs_2_, bf16[512,768]{1,0:T(8,128)(2,1)S(1)} %get-tuple-element.19.mix.refs_3_, ...), custom_call_target="tpu_custom_call" | custom-call | flops 805306368 | bytes 1048576 | tf_op jit(solution)/shard_map/round_rest/pallas_call | solution.py:130
  39.8 3.6 %collective-permute-start.4 = (bf16[128,512]{1,0:T(8,128)(2,1)S(1)}, bf16[128,512]{1,0:T(8,128)(2,1)S(1)}, u32[]{:S(2)}, u32[]{:S(2)}) collective-permute-start(bf16[128,512]{1,0:T(8,128)(2,1)S(1)} %get-tuple-element.34), channel_id=1, source_target_pairs={{0,15},{1,2},{2,1},{3,4},{4,3},{5,6},{6,5},{7,8},{8,7},{9,10},{10,... | collective-permute-start | bytes 393224 | tf_op jit(solution)/shard_map/ppermute | solution.py:219
  43.4 0.7 %local_part.3 = (f32[512,512]{1,0:T(8,128)S(1)}, f32[512,512]{1,0:T(8,128)S(1)}) custom-call(bf16[512,512]{1,0:T(8,128)(2,1)S(1)} %get-tuple-element.23.normed, bf16[512,512]{1,0:T(8,128)(2,1)S(1)} %get-tuple-element.31.w_self, bf16[512,768]{1,0:T(8,128)(2,1)S(1)} %get-tuple-element.19.mix.refs_3_), custom_call_target="tpu_custom_call" | custom-call | flops 536870912 | bytes 1048576 | tf_op jit(solution)/shard_map/local_part/pallas_call | solution.py:130
  44.1 2.8 %collective-permute-done.4.refs_4_ = bf16[128,512]{1,0:T(8,128)(2,1)S(1)} collective-permute-done((bf16[128,512]{1,0:T(8,128)(2,1)S(1)}, bf16[128,512]{1,0:T(8,128)(2,1)S(1)}, u32[]{:S(2)}, u32[]{:S(2)}) %collective-permute-start.4) | collective-permute-done | bytes 131104 | tf_op jit(solution)/shard_map/ppermute | solution.py:219
  46.9 3.1 %round_rest.3 = bf16[4,128,512]{2,1,0:T(8,128)(2,1)} custom-call(s32[1,2]{1,0:T(1,128)S(1)} %copy-done.6, f32[512,512]{1,0:T(8,128)S(1)} %get-tuple-element.24.refs_1_, f32[512,512]{1,0:T(8,128)S(1)} %get-tuple-element.25.refs_2_, bf16[512,768]{1,0:T(8,128)(2,1)S(1)} %get-tuple-element.19.mix.refs_3_, bf16[128,512]{1,0:T(8,128)(2,1)S(1)} %collective-permute-done.4.refs_4_, ...), custom_call_target="tpu_custom_call" | custom-call | flops 805306368 | bytes 1048576 | tf_op jit(solution)/shard_map/round_rest/pallas_call | solution.py:130
  (26 shorter events, 0.1 us)
Async XLA Ops:
  0.7 2.2 %copy-start = (bf16[32,128,512]{2,1,0:T(8,128)(2,1)S(1)}, bf16[32,128,512]{2,1,0:T(8,128)(2,1)}, u32[]{:S(2)}) copy-start(bf16[32,128,512]{2,1,0:T(8,128)(2,1)} %refs_3_.5) | copy-start | bytes 12582916
  2.8 1.2 %copy-start.1 = (bf16[32,128,128]{2,1,0:T(8,128)(2,1)S(1)}, bf16[32,128,128]{2,1,0:T(8,128)(2,1)}, u32[]{:S(2)}) copy-start(bf16[32,128,128]{2,1,0:T(8,128)(2,1)} %refs_4_.5) | copy-start | bytes 3145732
  4.1 0.7 %copy-start.4 = (s32[32]{0:T(128)S(1)}, s32[32]{0:T(128)}, u32[]{:S(2)}) copy-start(s32[32]{0:T(128)} %refs_0_.7) | copy-start | bytes 388
  4.7 0.7 %copy-start.5 = (s32[32]{0:T(128)S(1)}, s32[32]{0:T(128)}, u32[]{:S(2)}) copy-start(s32[32]{0:T(128)} %refs_1_.5) | copy-start | bytes 388
  10.5 17.2 %collective-permute-start = (bf16[4,128,512]{2,1,0:T(8,128)(2,1)S(1)}, bf16[4,128,512]{2,1,0:T(8,128)(2,1)S(1)}, u32[]{:S(2)}, u32[]{:S(2)}) collective-permute-start(bf16[4,128,512]{2,1,0:T(8,128)(2,1)S(1)} %pairs_on.1), channel_id=1, source_target_pairs={{0,1},{1,0},{2,3},{3,2},{4,5},{5,4},{6,7},{7,6},{8,9},{9,8},{10,11... | collective-permute-start | bytes 1572872 | tf_op jit(solution)/shard_map/ppermute | solution.py:222
  16.3 9.2 %copy-start.6 = (s32[1,2]{1,0:T(1,128)S(1)}, s32[1,2]{1,0:T(1,128)}, u32[]{:S(2)}) copy-start(s32[1,2]{1,0:T(1,128)} %refs_0_.9) | copy-start | bytes 28
  16.3 9.2 %copy-start.7 = (bf16[4,128,512]{2,1,0:T(8,128)(2,1)S(1)}, bf16[4,128,512]{2,1,0:T(8,128)(2,1)}, u32[]{:S(2)}) copy-start(bf16[4,128,512]{2,1,0:T(8,128)(2,1)} %state.1) | copy-start | bytes 1572868
  16.3 9.2 %copy-start.8 = (bf16[512,512]{1,0:T(8,128)(2,1)S(1)}, bf16[512,512]{1,0:T(8,128)(2,1)}, u32[]{:S(2)}) copy-start(bf16[512,512]{1,0:T(8,128)(2,1)} %w_self.1) | copy-start | bytes 1572868
  16.3 9.2 %copy-start.9 = (bf16[4,4,128,128]{3,2,1,0:T(8,128)(2,1)S(1)}, bf16[4,4,128,128]{3,2,1,0:T(8,128)(2,1)}, u32[]{:S(2)}) copy-start(bf16[4,4,128,128]{3,2,1,0:T(8,128)(2,1)} %coupling.1) | copy-start | bytes 1572868
  16.4 9.2 %copy-start.10 = (s32[4,4]{1,0:T(4,128)S(1)}, s32[4,4]{1,0:T(4,128)}, u32[]{:S(2)}) copy-start(s32[4,4]{1,0:T(4,128)} %nbr.1) | copy-start | bytes 196
  16.4 9.2 %copy-start.11 = (f32[512]{0:T(512)S(1)}, f32[512]{0:T(512)}, u32[]{:S(2)}) copy-start(f32[512]{0:T(512)} %param.26) | copy-start | bytes 6148
  16.4 11.1 %copy-start.15 = (f32[2,512]{1,0:T(2,128)S(1)}, f32[2,512]{1,0:T(2,128)}, u32[]{:S(2)}) copy-start(f32[2,512]{1,0:T(2,128)} %param.30) | copy-start | bytes 12292
  16.4 11.1 %copy-start.13 = (bf16[2,512,512]{2,1,0:T(8,128)(2,1)S(1)}, bf16[2,512,512]{2,1,0:T(8,128)(2,1)}, u32[]{:S(2)}) copy-start(bf16[2,512,512]{2,1,0:T(8,128)(2,1)} %param.33) | copy-start | bytes 3145732
  16.4 11.1 %copy-start.14 = (bf16[2,512,512]{2,1,0:T(8,128)(2,1)S(1)}, bf16[2,512,512]{2,1,0:T(8,128)(2,1)}, u32[]{:S(2)}) copy-start(bf16[2,512,512]{2,1,0:T(8,128)(2,1)} %param.32) | copy-start | bytes 3145732
  16.4 11.5 %collective-permute-start.1 = (bf16[4,128,512]{2,1,0:T(8,128)(2,1)S(1)}, bf16[4,128,512]{2,1,0:T(8,128)(2,1)S(1)}, u32[]{:S(2)}, u32[]{:S(2)}) collective-permute-start(bf16[4,128,512]{2,1,0:T(8,128)(2,1)S(1)} %pairs_off.1), channel_id=1, source_target_pairs={{0,15},{1,2},{2,1},{3,4},{4,3},{5,6},{6,5},{7,8},{8,7},{9,10},{10,... | collective-permute-start | bytes 1572872 | tf_op jit(solution)/shard_map/ppermute | solution.py:219
  25.5 2.4 %copy-start.2 = (bf16[512,512]{1,0:T(8,128)(2,1)S(1)}, bf16[512,512]{1,0:T(8,128)(2,1)}, u32[]{:S(2)}) copy-start(bf16[512,512]{1,0:T(8,128)(2,1)} %w_obs.1) | copy-start | bytes 1572868
  25.5 2.4 %copy-start.3 = (bf16[512,512]{1,0:T(8,128)(2,1)S(1)}, bf16[512,512]{1,0:T(8,128)(2,1)}, u32[]{:S(2)}) copy-start(bf16[512,512]{1,0:T(8,128)(2,1)} %w_out.1) | copy-start | bytes 1572868
  27.5 6.0 %copy-start.12 = (bf16[2,512,512]{2,1,0:T(8,128)(2,1)S(1)}, bf16[2,512,512]{2,1,0:T(8,128)(2,1)}, u32[]{:S(2)}) copy-start(bf16[2,512,512]{2,1,0:T(8,128)(2,1)} %param.31) | copy-start | bytes 3145732
  30.0 7.2 %collective-permute-start.2 = (bf16[128,512]{1,0:T(8,128)(2,1)S(1)}, bf16[128,512]{1,0:T(8,128)(2,1)S(1)}, u32[]{:S(2)}, u32[]{:S(2)}) collective-permute-start(bf16[128,512]{1,0:T(8,128)(2,1)S(1)} %get-tuple-element.36), channel_id=1, source_target_pairs={{0,15},{1,2},{2,1},{3,4},{4,3},{5,6},{6,5},{7,8},{8,7},{9,10},{10,... | collective-permute-start | bytes 393224 | tf_op jit(solution)/shard_map/ppermute | solution.py:219
  33.5 3.6 %collective-permute-start.3 = (bf16[128,512]{1,0:T(8,128)(2,1)S(1)}, bf16[128,512]{1,0:T(8,128)(2,1)S(1)}, u32[]{:S(2)}, u32[]{:S(2)}) collective-permute-start(bf16[128,512]{1,0:T(8,128)(2,1)S(1)} %get-tuple-element.35), channel_id=1, source_target_pairs={{0,1},{1,0},{2,3},{3,2},{4,5},{5,4},{6,7},{7,6},{8,9},{9,8},{10,11... | collective-permute-start | bytes 393224 | tf_op jit(solution)/shard_map/ppermute | solution.py:222
  39.8 7.2 %collective-permute-start.4 = (bf16[128,512]{1,0:T(8,128)(2,1)S(1)}, bf16[128,512]{1,0:T(8,128)(2,1)S(1)}, u32[]{:S(2)}, u32[]{:S(2)}) collective-permute-start(bf16[128,512]{1,0:T(8,128)(2,1)S(1)} %get-tuple-element.34), channel_id=1, source_target_pairs={{0,15},{1,2},{2,1},{3,4},{4,3},{5,6},{6,5},{7,8},{8,7},{9,10},{10,... | collective-permute-start | bytes 393224 | tf_op jit(solution)/shard_map/ppermute | solution.py:219
  43.4 3.5 %collective-permute-start.5 = (bf16[128,512]{1,0:T(8,128)(2,1)S(1)}, bf16[128,512]{1,0:T(8,128)(2,1)S(1)}, u32[]{:S(2)}, u32[]{:S(2)}) collective-permute-start(bf16[128,512]{1,0:T(8,128)(2,1)S(1)} %get-tuple-element.33), channel_id=1, source_target_pairs={{0,1},{1,0},{2,3},{3,2},{4,5},{5,4},{6,7},{7,6},{8,9},{9,8},{10,11... | collective-permute-start | bytes 393224 | tf_op jit(solution)/shard_map/ppermute | solution.py:222

commit v2 on v1

v2 whole, which is shorter than its diff:
```python
import jax
import jax.numpy as jnp
from jax import lax
from jax.experimental import pallas as pl
from jax.experimental.pallas import tpu as pltpu
from jax.sharding import PartitionSpec as P

F32 = jnp.float32
BF16 = jnp.bfloat16
VMEM = pl.BlockSpec(memory_space=pltpu.VMEM)
SMEM = pl.BlockSpec(memory_space=pltpu.SMEM)
HBM = pl.BlockSpec(memory_space=pltpu.HBM)


def dot(a, b):
    return jnp.dot(a, b, preferred_element_type=F32)


def silu(v):
    half = 0.5 * v
    return half + half * jnp.tanh(half)


def norm_rows(values, gain):
    center = values - jnp.mean(values, axis=-1, keepdims=True)
    spread = jnp.mean(center * center, axis=-1, keepdims=True)
    return (center * lax.rsqrt(spread + 1e-05) * gain).astype(BF16)


def odd_device():
    return lax.rem(lax.axis_index("mesh"), 2)


def block_order(rim):
    odd = odd_device()
    off = rim[0, odd]
    on = rim[0, 1 - odd]
    low = jnp.minimum(off, on)
    high = jnp.maximum(off, on)
    third = jnp.where(low > 0, 0, jnp.where(high > 1, 1, 2))
    fourth = jnp.where(high < 3, 3, jnp.where(low < 2, 2, 1))
    return [off, on, third, fourth]


def pair_kernel(sides, cnt, tgt_hbm, src_hbm, obs, cpl, *refs):
    outs = refs[: len(sides)]
    tgt, src, isem, xbuf, cbuf, acc, xsem, csem = refs[-8:]
    blocks = outs[0].shape[0]
    odd = odd_device()
    parts = [{"off": 2 * odd, "on": 2 - 2 * odd, "self": 1}[side] for side in sides]
    reads = [
        pltpu.make_async_copy(a, b, isem.at[i])
        for i, (a, b) in enumerate(((tgt_hbm, tgt), (src_hbm, src)))
    ]
    for read in reads:
        read.start()
    for read in reads:
        read.wait()
    live = cnt[0]

    def group(e):
        t = tgt[e]
        mine, place = jnp.bool_(False), jnp.int32(0)
        for i, part in enumerate(parts):
            here = (t >= part * blocks) & (t < (part + 1) * blocks)
            mine = mine | here
            place = jnp.where(here, t - part * blocks + i * blocks, place)
        return place, mine

    groups = len(sides) * blocks

    def bump(words, place, mine):
        return [
            word + jnp.where(mine & (place // 4 == i), 1 << (8 * (place % 4)), 0)
            for i, word in enumerate(words)
        ]

    def count(e, words):
        return bump(words, *group(e))

    words = lax.fori_loop(0, live, count, [jnp.int32(0)] * (groups // 4))
    counts = [(words[g // 4] >> (8 * (g % 4))) & 255 for g in range(groups)]
    firsts, total = [], jnp.int32(0)
    for g in range(groups):
        firsts.append(total)
        total = total + counts[g]
    free = []
    for i in range(groups // 4):
        word = jnp.int32(0)
        for j in range(4):
            word = word + (firsts[4 * i + j] << (8 * j))
        free.append(word)

    def fetch(e, words):
        place, mine = group(e)
        word = words[0]
        for i in range(1, len(words)):
            word = jnp.where(place // 4 == i, words[i], word)

        @pl.when(mine)
        def _():
            slot = (word >> (8 * (place % 4))) & 255
            pltpu.make_async_copy(obs.at[src[e]], xbuf.at[slot], xsem.at[slot]).start()
            pltpu.make_async_copy(cpl.at[e], cbuf.at[slot], csem.at[slot]).start()

        return bump(words, place, mine)

    lax.fori_loop(0, live, fetch, free)

    def arrive(slot):
        pltpu.make_async_copy(obs.at[0], xbuf.at[slot], xsem.at[slot]).wait()
        pltpu.make_async_copy(cpl.at[0], cbuf.at[slot], csem.at[slot]).wait()

    for g in range(groups):
        acc[...] = jnp.zeros_like(acc)

        def two(j, carry):
            slot = firsts[g] + 2 * j
            arrive(slot)
            arrive(slot + 1)
            left = jnp.concatenate([cbuf[slot], cbuf[slot + 1]], axis=1)
            right = jnp.concatenate([xbuf[slot], xbuf[slot + 1]], axis=0)
            acc[...] += dot(left, right)
            return carry

        lax.fori_loop(0, counts[g] // 2, two, 0)

        @pl.when(counts[g] % 2 == 1)
        def _():
            slot = firsts[g] + counts[g] - 1
            arrive(slot)
            acc[...] += dot(cbuf[slot], xbuf[slot])

        out = outs[g // blocks]
        out[g % blocks] = acc[...].astype(out.dtype)


def pair_sums(sides, blocks, tgt, src, cnt, obs, cpl, after=None):
    slots, rows, width = tgt.shape[0], obs.shape[1], obs.shape[2]
    more = [] if after is None else [after]
    return pl.pallas_call(
        lambda *refs: pair_kernel(list(sides), *refs[:5], *refs[5 + len(more) :]),
        out_shape=[jax.ShapeDtypeStruct((blocks, rows, width), d) for d in sides.values()],
        in_specs=[SMEM] + [HBM] * 4 + [pl.BlockSpec(memory_space=pl.ANY)] * len(more),
        out_specs=[VMEM] * len(sides),
        scratch_shapes=[
            pltpu.SMEM((slots,), jnp.int32),
            pltpu.SMEM((slots,), jnp.int32),
            pltpu.SemaphoreType.DMA((2,)),
            pltpu.VMEM((slots, rows, width), BF16),
            pltpu.VMEM((slots, rows, rows), BF16),
            pltpu.VMEM((rows, width), F32),
            pltpu.SemaphoreType.DMA((slots,)),
            pltpu.SemaphoreType.DMA((slots,)),
        ],
        compiler_params=pltpu.CompilerParams(vmem_limit_bytes=12 << 20),
        cost_estimate=pl.CostEstimate(flops=1 << 20, bytes_accessed=1 << 30, transcendentals=0),
        name="pairs_" + "_".join(sides),
    )(cnt, *[pltpu.with_memory_space_constraint(x, pltpu.HBM) for x in (tgt, src, obs, cpl)], *more)


def call(kernel, out, scalars, arrays, name, weight=20):
    return pl.pallas_call(
        kernel,
        out_shape=out,
        in_specs=[SMEM] * len(scalars) + [VMEM] * len(arrays),
        out_specs=[VMEM] * len(out),
        compiler_params=pltpu.CompilerParams(vmem_limit_bytes=14 << 20),
        cost_estimate=pl.CostEstimate(flops=1 << weight, bytes_accessed=1 << 24, transcendentals=0),
        name=name,
    )(*scalars, *arrays)


def update(state, pre, incoming, w_in, w_out):
    hidden = silu(pre + dot(incoming, w_in)).astype(BF16)
    return (state.astype(F32) + dot(hidden, w_out)).astype(BF16)


def prepare_kernel(rim, nbr, state, gain, w_self, coupling, pre, state_p, mix):
    blocks, rows = state.shape[0], state.shape[1]
    order = block_order(rim)
    odd = odd_device()
    last = blocks + 1
    codes = [1 + o for o in order] + [last * odd, last - last * odd]
    for i, m in enumerate(order):
        cut = pl.ds(i * rows, rows)
        values = state[m]
        state_p[cut, :] = values
        pre[cut, :] = dot(norm_rows(values.astype(F32), gain[...]), w_self[...])
        for c, code in enumerate(codes):
            total = None
            for k in range(coupling.shape[1]):
                term = jnp.where(nbr[m, k] == code, coupling[m, k].astype(F32), 0.0)
                total = term if total is None else total + term
            mix[cut, c * rows : (c + 1) * rows] = total.astype(BF16)


def pack_kernel(rim, state_p, own, on, mix, packed):
    rows, width = own.shape[1], own.shape[2]
    size = state_p.shape[0]
    m = block_order(rim)[0]
    packed[:, :width] = state_p[:rows, :]
    packed[:, width : 2 * width] = (own[m] + on[m].astype(F32)).astype(BF16)
    packed[:, 2 * width : 2 * width + rows] = mix[:rows, size : size + rows]
    lane = lax.broadcasted_iota(jnp.int32, (rows, 128), 1)
    packed[:, 2 * width + rows :] = jnp.where(lane == m, 1.0, 0.0).astype(BF16)


def encode_kernel(half, rim, pre, state_p, own, on, off, w_obs, w_out, gain, state, normed, *rims):
    rows = own.shape[1]
    summed = jnp.concatenate(
        [
            (own[m] + on[m].astype(F32) + off[m].astype(F32)).astype(BF16)
            for m in block_order(rim)[2 * half : 2 * half + 2]
        ],
        axis=0,
    )
    cut = slice(2 * half * rows, 2 * (half + 1) * rows)
    updated = update(state_p[cut, :], pre[cut, :], summed, w_obs[...], w_out[...])
    state[...] = updated
    result = norm_rows(updated.astype(F32), gain[:1, :])
    normed[...] = result
    if rims:
        rims[0][...] = result[rows:, :]


def partial_kernel(mix, first, second, on, message):
    rows, size = on.shape[0], mix.shape[0]
    message[...] = (
        dot(mix[:rows, : 2 * rows], first[...])
        + dot(mix[:rows, 2 * rows : size], second[...])
        + dot(mix[:rows, size + rows :], on[...])
    ).astype(BF16)


def neighbour_kernel(packed, sent, first, gain, w_self, w_obs, w_out, node_gain, n_self, _, state, normed, pre, message):
    rows, width = state.shape
    own = packed[:, :width]
    summed = packed[:, width : 2 * width].astype(F32)
    for t in range(sent.shape[0]):
        mask = packed[:, 2 * width + rows + t : 2 * width + rows + t + 1].astype(F32)
        summed = summed + mask * sent[t].astype(F32)
    start = dot(norm_rows(own.astype(F32), gain[...]), w_self[...])
    updated = update(own, start, summed.astype(BF16), w_obs[...], w_out[...])
    state[...] = updated
    result = norm_rows(updated.astype(F32), node_gain[:1, :])
    normed[...] = result
    pre[...] = dot(result, n_self[0])
    message[...] = dot(packed[:, 2 * width : 2 * width + rows], first[:rows, :])


def round_kernel(mix, first, second, off, on, state_a, state_b, n_self, n_msg, n_out, gain, state, normed, rim):
    size = state.shape[0]
    rows = off.shape[0]
    heard = jnp.concatenate([first[...], second[...], off[...], on[...]], axis=0)
    for half, (base, own) in enumerate(((state_a, first), (state_b, second))):
        cut = slice(2 * half * rows, 2 * (half + 1) * rows)
        incoming = dot(mix[cut, :], heard).astype(BF16)
        updated = update(base[...], dot(own[...], n_self[0]), incoming, n_msg[0], n_out[0])
        state[cut, :] = updated
        result = norm_rows(updated.astype(F32), gain[1:2, :])
        normed[cut, :] = result
        if half == 0:
            rim[...] = result[rows:, :]


def local_kernel(mix, normed, n_self, pre, message):
    size = normed.shape[0]
    pre[...] = dot(normed[...], n_self[1])
    message[...] = dot(mix[:, :size], normed[...])


def last_kernel(
    rim, arrived, on, far_message, far_pre, far_state, mix, pre, message, state, n_msg, n_out, gain, out
):
    rows = arrived.shape[0]
    size = state.shape[0]
    incoming = (arrived[...].astype(F32) + far_message[...]).astype(BF16)
    far = update(far_state[...], far_pre[...], incoming, n_msg[0], n_out[0])
    far = norm_rows(far.astype(F32), gain[1:2, :])
    rims = jnp.concatenate([far, on[...]], axis=0)
    order = block_order(rim)
    for half in range(2):
        cut = slice(2 * half * rows, 2 * (half + 1) * rows)
        incoming = (message[cut, :] + dot(mix[cut, size:], rims)).astype(BF16)
        updated = update(state[cut, :], pre[cut, :], incoming, n_msg[1], n_out[1])
        out[order[2 * half]] = updated[:rows, :]
        out[order[2 * half + 1]] = updated[rows:, :]


def shards(
    mesh_state,
    obs_latent,
    pair_coupling,
    pair_target,
    pair_source,
    pair_count,
    mesh_coupling,
    neighbor,
    rim_send,
    enc_gain,
    enc_self,
    enc_obs,
    enc_out,
    node_gain,
    node_self,
    node_msg,
    node_out,
):
    blocks, rows, width = mesh_state.shape
    size = blocks * rows
    count = lax.axis_size("mesh")
    on_route = [(i, i ^ 1) for i in range(count)]
    off_route = [(i, (i + 1) % count if i % 2 else (i - 1) % count) for i in range(count)]

    def swap_off(x):
        return lax.ppermute(x, "mesh", off_route)

    def swap_on(x):
        return lax.ppermute(x, "mesh", on_route)

    def wide(n, dtype=BF16):
        return jax.ShapeDtypeStruct((n, width), dtype)

    enc_gain = enc_gain[None]
    pairs = (pair_target, pair_source, pair_count, obs_latent, pair_coupling)
    (sent,) = pair_sums({"off": BF16}, blocks, *pairs)
    sums_off = swap_off(sent)
    sent_on, sums_own = pair_sums({"on": BF16, "self": F32}, blocks, *pairs, after=sent)
    sums_on = swap_on(sent_on)
    pre, state_p, mix = call(
        prepare_kernel,
        [wide(size, F32), wide(size), jax.ShapeDtypeStruct((size, size + 2 * rows), BF16)],
        [rim_send, neighbor],
        [mesh_state, enc_gain, enc_self, mesh_coupling],
        "prepare",
        weight=40,
    )
    (packed,) = call(
        pack_kernel,
        [jax.ShapeDtypeStruct((rows, 2 * width + 2 * rows), BF16)],
        [rim_send],
        [state_p, sums_own, sums_on, mix],
        "pack",
    )
    packed = swap_off(packed)
    encode = (pre, state_p, sums_own, sums_on, sums_off, enc_obs, enc_out, node_gain)
    state_a, first, rim_on = call(
        lambda *refs: encode_kernel(0, *refs),
        [wide(2 * rows), wide(2 * rows), wide(rows)],
        [rim_send],
        encode,
        "encode_rims",
    )
    on = swap_on(rim_on)
    state_b, second = call(
        lambda *refs: encode_kernel(1, *refs),
        [wide(2 * rows), wide(2 * rows)],
        [rim_send],
        encode,
        "encode_others",
    )
    (message,) = call(partial_kernel, [wide(rows)], [], [mix, first, second, on], "rim_message")
    arrived = swap_off(message)
    far_state, far, far_pre, far_message = call(
        neighbour_kernel,
        [wide(rows), wide(rows), wide(rows, F32), wide(rows, F32)],
        [],
        [packed, sent, first, enc_gain, enc_self, enc_obs, enc_out, node_gain, node_self, message],
        "neighbour_rim",
    )
    state, normed, rim_on = call(
        round_kernel,
        [wide(size), wide(size), wide(rows)],
        [],
        [mix, first, second, far, on, state_a, state_b, node_self, node_msg, node_out, node_gain],
        "round_0",
    )
    on = swap_on(rim_on)
    pre, message = call(
        local_kernel,
        [wide(size, F32), wide(size, F32)],
        [],
        [mix, normed, node_self],
        "round_1_local",
    )
    (out,) = call(
        last_kernel,
        [jax.ShapeDtypeStruct((blocks, rows, width), BF16)],
        [rim_send],
        [arrived, on, far_message, far_pre, far_state, mix, pre, message, state, node_msg, node_out, node_gain],
        "round_1",
    )
    return out


def solution(mesh):
    block = P(("groups", "mesh"), None, None)
    return jax.shard_map(
        shards,
        mesh=mesh,
        in_specs=(
            block,
            block,
            block,
            P(("groups", "mesh")),
            P(("groups", "mesh")),
            P(("groups", "mesh")),
            P("mesh", None, None, None),
            P("mesh", None),
            P("mesh", None),
        )
        + (P(),) * 8,
        out_specs=block,
        check_vma=False,
    )
```

time: 50.5 us -> 40.9 us (0.81); the launches traced: 50 us -> 41.5 us
  starting transfers between devices: 10.7 us -> 15.9 us
  waiting for transfers between devices: 5.92 us -> 0.86 us
  local copies, waits for them, and re-layouts: 5.04 us -> 0.08 us
  Pallas kernels: 27.4 us -> 23.7 us
    ppermute x3, waiting for transfers between devices: 5.91 us -> 0.01 us  [swap_off(): return lax.ppermute(x, 'mesh', off_route)]
    ppermute x3, starting transfers between devices: 10.6 us -> 15.7 us  [swap_off(): return lax.ppermute(x, 'mesh', off_route)]
    unnamed x32 -> x24, local copies, waits for them, and re-layouts: 4.79 us -> 0.08 us
    pallas_call x9 -> x11, Pallas kernels: 27.4 us -> 23.7 us  [the longest x9 15.4 us: call(): pl.pallas_call(kernel, out_shape=out, in_specs=[SMEM] * len(scalars) + [V...]
    ppermute x3, waiting for transfers between devices: 0.01 us -> 0.85 us  [swap_on(): return lax.ppermute(x, 'mesh', on_route)]
  transfers between devices with their start and end apart: 6 -> 6, of which waited for: 3 -> 2; matrix products, arithmetic and copies ran while one was open for 0% -> 0% of each run, Pallas kernels for 29% -> 41%
where the time goes in v2:
time: 40.9 us; the launch traced here: 41.5 us
  Pallas kernels  23.7 us (58%)
  starting transfers between devices  15.9 us (39%)
  between operations  0.93 us (2%)
  waiting for transfers between devices  0.86 us (2%)
    ppermute x3, starting transfers between devices, swap_off(): return lax.ppermute(x, 'mesh', off_route)  15.7 us
    pallas_call x9, Pallas kernels, call(): pl.pallas_call(kernel, out_shape=out, in_specs=[SMEM] * len(scalars) + [V...  15.4 us
    pallas_call x2, Pallas kernels, pair_sums(): pl.pallas_call(lambda *refs: pair_kernel(list(sides), *refs[:5], *refs[5...  8.34 us
    ppermute x3, waiting for transfers between devices, swap_on(): return lax.ppermute(x, 'mesh', on_route)  0.85 us
  transfers between devices with their start and end apart: 6, of which 2 were waited for; matrix products, arithmetic and copies ran while one was open for 0% of the time, Pallas kernels for 41%

profile of v2, /device:TPU:0, one launch (start us, length us, event | category | flops | bytes accessed | tf_op | source)
XLA Modules:
  0.0 41.5 jit_solution(5286562574983733869)
XLA Ops:
  0.7 3.4 %pairs_off.1.refs_5_.sent = bf16[4,128,512]{2,1,0:T(8,128)(2,1)} custom-call(s32[1]{0:T(128)S(6)} %copy.18.refs_0_, s32[32]{0:T(128)} %refs_1_.3, s32[32]{0:T(128)} %refs_2_.3, bf16[32,128,512]{2,1,0:T(8,128)(2,1)} %refs_3_.3, bf16[32,128,128]{2,1,0:T(8,128)(2,1)} %refs_4_.3), custom_call_target="tpu_custom_call" | custom-call | flops 1048576 | bytes 1073741824 | tf_op jit(solution)/shard_map/pairs_off/pallas_call | solution.py:141
  4.0 0.0 copy-start.5
  4.0 0.0 copy-start.7
  4.0 0.0 copy-start.8
  4.1 0.0 copy-start.9
  4.1 0.0 copy-start.10
  4.1 0.0 copy-start.11
  4.1 7.1 %collective-permute-start.1 = (bf16[4,128,512]{2,1,0:T(8,128)(2,1)}, bf16[4,128,512]{2,1,0:T(8,128)(2,1)}, u32[]{:S(2)}, u32[]{:S(2)}) collective-permute-start(bf16[4,128,512]{2,1,0:T(8,128)(2,1)} %pairs_off.1.refs_5_.sent), channel_id=1, source_target_pairs={{0,15},{1,2},{2,1},{3,4},{4,3},{5,6},{6,5},{7,8},{8,7},{9,10},{10,... | collective-permute-start | bytes 1572872 | tf_op jit(solution)/shard_map/ppermute | solution.py:317
  11.2 5.0 %pairs_on_self.1 = (bf16[4,128,512]{2,1,0:T(8,128)(2,1)}, f32[4,128,512]{2,1,0:T(8,128)S(1)}) custom-call(s32[1]{0:T(128)S(6)} %copy.18.refs_0_, s32[32]{0:T(128)} %refs_1_.3, s32[32]{0:T(128)} %refs_2_.3, bf16[32,128,512]{2,1,0:T(8,128)(2,1)} %refs_3_.3, bf16[32,128,128]{2,1,0:T(8,128)(2,1)} %refs_4_.3, bf16[4,128,512]{2,1,0:T(8,128)(2,1)} %pairs_off.1.refs_5_.sent), custom_call_target="tpu_custom_call" | custom-call | flops 1048576 | bytes 1073741824 | tf_op jit(solution)/shard_map/pairs_on_self/pallas_call | solution.py:141
  16.2 0.1 collective-permute-start
  16.3 0.0 copy-start.1
  16.3 0.0 copy-start.2
  16.3 0.0 copy-start.6
  16.4 1.9 %prepare.1 = (f32[512,512]{1,0:T(8,128)S(1)}, bf16[512,512]{1,0:T(8,128)(2,1)S(1)}, bf16[512,768]{1,0:T(8,128)(2,1)S(1)}) custom-call(s32[1,2]{1,0:T(1,128)S(1)} %copy-done.7, s32[4,4]{1,0:T(4,128)S(1)} %copy-done.11, bf16[4,128,512]{2,1,0:T(8,128)(2,1)S(1)} %copy-done.9, f32[1,512]{1,0:T(1,128)S(1)} %bitcast.1, bf16[512,512]{1,0:T(8,128)(2,1)S(1)} %copy-done.5, ...), custom_call_target="tpu_custom_call" | custom-call | flops 1099511627776 | bytes 16777216 | tf_op jit(solution)/shard_map/prepare/pallas_call | solution.py:163
  18.3 0.2 collective-permute-done.refs_4_.on
  18.5 1.1 %pack.1 = bf16[128,1280]{1,0:T(8,128)(2,1)S(1)} custom-call(s32[1,2]{1,0:T(1,128)S(1)} %copy-done.7, bf16[512,512]{1,0:T(8,128)(2,1)S(1)} %get-tuple-element.26.refs_2_.state_p, f32[4,128,512]{2,1,0:T(8,128)S(1)} %get-tuple-element.27.refs_3_.own, bf16[4,128,512]{2,1,0:T(8,128)(2,1)} %collective-permute-done.refs_4_.on, ...), custom_call_target="tpu_custom_call" | custom-call | flops 1048576 | bytes 16777216 | tf_op jit(solution)/shard_map/pack/pallas_call | solution.py:163
  19.6 3.3 %collective-permute-start.4 = (bf16[128,1280]{1,0:T(8,128)(2,1)S(1)}, bf16[128,1280]{1,0:T(8,128)(2,1)S(1)}, u32[]{:S(2)}, u32[]{:S(2)}) collective-permute-start(bf16[128,1280]{1,0:T(8,128)(2,1)S(1)} %pack.1), channel_id=1, source_target_pairs={{0,15},{1,2},{2,1},{3,4},{4,3},{5,6},{6,5},{7,8},{8,7},{9,10},{10,... | collective-permute-start | bytes 983048 | tf_op jit(solution)/shard_map/ppermute | solution.py:317
  22.9 0.0 collective-permute-done.1.refs_5_
  23.0 2.0 %encode_rims.1 = (bf16[256,512]{1,0:T(8,128)(2,1)S(1)}, bf16[256,512]{1,0:T(8,128)(2,1)S(1)}, bf16[128,512]{1,0:T(8,128)(2,1)S(1)}) custom-call(s32[1,2]{1,0:T(1,128)S(1)} %copy-done.7, f32[512,512]{1,0:T(8,128)S(1)} %get-tuple-element.25.refs_1_, bf16[512,512]{1,0:T(8,128)(2,1)S(1)} %get-tuple-element.26.refs_2_.state_p, ...), custom_call_target="tpu_custom_call" | custom-call | flops 1048576 | bytes 16777216 | tf_op jit(solution)/shard_map/encode_rims/pallas_call | solution.py:163
  24.9 0.0 copy-start
  25.0 0.0 copy-start.3
  25.0 0.0 copy-start.4
  25.0 0.1 collective-permute-start.2
  25.1 2.1 %encode_others.1 = (bf16[256,512]{1,0:T(8,128)(2,1)S(1)}, bf16[256,512]{1,0:T(8,128)(2,1)S(1)}) custom-call(s32[1,2]{1,0:T(1,128)S(1)} %copy-done.7, f32[512,512]{1,0:T(8,128)S(1)} %get-tuple-element.25.refs_1_, bf16[512,512]{1,0:T(8,128)(2,1)S(1)} %get-tuple-element.26.refs_2_.state_p, f32[4,128,512]{2,1,0:T(8,128)S(1)} %get-tuple-element.27.refs_3_.own, ...), custom_call_target="tpu_custom_call" | custom-call | flops 1048576 | bytes 16777216 | tf_op jit(solution)/shard_map/encode_others/pallas_call | solution.py:163
  27.2 0.3 rim_message.1._
  27.5 5.2 %collective-permute-start.3 = (bf16[128,512]{1,0:T(8,128)(2,1)S(1)}, bf16[128,512]{1,0:T(8,128)(2,1)S(1)}, u32[]{:S(2)}, u32[]{:S(2)}) collective-permute-start(bf16[128,512]{1,0:T(8,128)(2,1)S(1)} %rim_message.1._), channel_id=1, source_target_pairs={{0,15},{1,2},{2,1},{3,4},{4,3},{5,6},{6,5},{7,8},{8,7},{9,10},{10,... | collective-permute-start | bytes 393224 | tf_op jit(solution)/shard_map/ppermute | solution.py:317
  32.7 2.2 %neighbour_rim.1 = (bf16[128,512]{1,0:T(8,128)(2,1)S(1)}, bf16[128,512]{1,0:T(8,128)(2,1)S(1)}, f32[128,512]{1,0:T(8,128)S(1)}, f32[128,512]{1,0:T(8,128)S(1)}) custom-call(bf16[128,1280]{1,0:T(8,128)(2,1)S(1)} %collective-permute-done.4.packed, bf16[4,128,512]{2,1,0:T(8,128)(2,1)} %pairs_off.1.refs_5_.sent, bf16[256,512]{1,0:T(8,128)(2,1)S(1)} %get-tuple-element.29.first, ...), custom_call_target="tpu_custom_call" | custom-call | flops 1048576 | bytes 16777216 | tf_op jit(solution)/shard_map/neighbour_rim/pallas_call | solution.py:163
  34.9 2.0 %round_0.1 = (bf16[512,512]{1,0:T(8,128)(2,1)S(1)}, bf16[512,512]{1,0:T(8,128)(2,1)S(1)}, bf16[128,512]{1,0:T(8,128)(2,1)S(1)}) custom-call(bf16[512,768]{1,0:T(8,128)(2,1)S(1)} %get-tuple-element.24.mix, bf16[256,512]{1,0:T(8,128)(2,1)S(1)} %get-tuple-element.29.first, bf16[256,512]{1,0:T(8,128)(2,1)S(1)} %get-tuple-element.30.second, ...), custom_call_target="tpu_custom_call" | custom-call | flops 1048576 | bytes 16777216 | tf_op jit(solution)/shard_map/round_0/pallas_call | solution.py:163
  36.9 0.1 collective-permute-start.5
  37.0 0.7 %round_1_local.1 = (f32[512,512]{1,0:T(8,128)S(1)}, f32[512,512]{1,0:T(8,128)S(1)}) custom-call(bf16[512,768]{1,0:T(8,128)(2,1)S(1)} %get-tuple-element.24.mix, bf16[512,512]{1,0:T(8,128)(2,1)S(1)} %get-tuple-element.39.normed, bf16[2,512,512]{2,1,0:T(8,128)(2,1)S(1)} %copy-done), custom_call_target="tpu_custom_call" | custom-call | flops 1048576 | bytes 16777216 | tf_op jit(solution)/shard_map/round_1_local/pallas_call | solution.py:163
  37.7 0.6 %collective-permute-done.5.on = bf16[128,512]{1,0:T(8,128)(2,1)S(1)} collective-permute-done((bf16[128,512]{1,0:T(8,128)(2,1)S(1)}, bf16[128,512]{1,0:T(8,128)(2,1)S(1)}, u32[]{:S(2)}, u32[]{:S(2)}) %collective-permute-start.5) | collective-permute-done | bytes 131104 | tf_op jit(solution)/shard_map/ppermute | solution.py:320
  38.3 3.2 %round_1.1 = bf16[4,128,512]{2,1,0:T(8,128)(2,1)} custom-call(s32[1,2]{1,0:T(1,128)S(1)} %copy-done.7, bf16[128,512]{1,0:T(8,128)(2,1)S(1)} %collective-permute-done.3.arrived, bf16[128,512]{1,0:T(8,128)(2,1)S(1)} %collective-permute-done.5.on, f32[128,512]{1,0:T(8,128)S(1)} %get-tuple-element.36.far_message, f32[128,512]{1,0:T(8,128)S(1)} %get-tuple-element.37.far_pre, ...), custom_call_target="tpu_custom_call" | custom-call | flops 1048576 | bytes 16777216 | tf_op jit(solution)/shard_map/round_1/pallas_call | solution.py:163
  (15 shorter events, 0.0 us)
Async XLA Ops:
  4.0 12.2 %copy-start.5 = (bf16[512,512]{1,0:T(8,128)(2,1)S(1)}, bf16[512,512]{1,0:T(8,128)(2,1)}, u32[]{:S(2)}) copy-start(bf16[512,512]{1,0:T(8,128)(2,1)} %w_self.3) | copy-start | bytes 1572868
  4.0 12.2 %copy-start.7 = (s32[1,2]{1,0:T(1,128)S(1)}, s32[1,2]{1,0:T(1,128)}, u32[]{:S(2)}) copy-start(s32[1,2]{1,0:T(1,128)} %rim.5) | copy-start | bytes 28
  4.0 12.2 %copy-start.8 = (f32[512]{0:T(512)S(1)}, f32[512]{0:T(512)}, u32[]{:S(2)}) copy-start(f32[512]{0:T(512)} %param.26) | copy-start | bytes 6148
  4.1 12.2 %copy-start.9 = (bf16[4,128,512]{2,1,0:T(8,128)(2,1)S(1)}, bf16[4,128,512]{2,1,0:T(8,128)(2,1)}, u32[]{:S(2)}) copy-start(bf16[4,128,512]{2,1,0:T(8,128)(2,1)} %state.1) | copy-start | bytes 1572868
  4.1 12.2 %copy-start.10 = (bf16[4,4,128,128]{3,2,1,0:T(8,128)(2,1)S(1)}, bf16[4,4,128,128]{3,2,1,0:T(8,128)(2,1)}, u32[]{:S(2)}) copy-start(bf16[4,4,128,128]{3,2,1,0:T(8,128)(2,1)} %coupling.1) | copy-start | bytes 1572868
  4.1 12.2 %copy-start.11 = (s32[4,4]{1,0:T(4,128)S(1)}, s32[4,4]{1,0:T(4,128)}, u32[]{:S(2)}) copy-start(s32[4,4]{1,0:T(4,128)} %nbr.1) | copy-start | bytes 196
  4.1 18.9 %collective-permute-start.1 = (bf16[4,128,512]{2,1,0:T(8,128)(2,1)}, bf16[4,128,512]{2,1,0:T(8,128)(2,1)}, u32[]{:S(2)}, u32[]{:S(2)}) collective-permute-start(bf16[4,128,512]{2,1,0:T(8,128)(2,1)} %pairs_off.1.refs_5_.sent), channel_id=1, source_target_pairs={{0,15},{1,2},{2,1},{3,4},{4,3},{5,6},{6,5},{7,8},{8,7},{9,10},{10,... | collective-permute-start | bytes 1572872 | tf_op jit(solution)/shard_map/ppermute | solution.py:317
  16.2 2.3 %collective-permute-start = (bf16[4,128,512]{2,1,0:T(8,128)(2,1)}, bf16[4,128,512]{2,1,0:T(8,128)(2,1)}, u32[]{:S(2)}, u32[]{:S(2)}) collective-permute-start(bf16[4,128,512]{2,1,0:T(8,128)(2,1)} %get-tuple-element.28), channel_id=1, source_target_pairs={{0,1},{1,0},{2,3},{3,2},{4,5},{5,4},{6,7},{7,6},{8,9},{9,8},{10,11... | collective-permute-start | bytes 1572872 | tf_op jit(solution)/shard_map/ppermute | solution.py:320
  16.3 6.6 %copy-start.1 = (bf16[512,512]{1,0:T(8,128)(2,1)S(1)}, bf16[512,512]{1,0:T(8,128)(2,1)}, u32[]{:S(2)}) copy-start(bf16[512,512]{1,0:T(8,128)(2,1)} %w_obs.1) | copy-start | bytes 1572868
  16.3 6.6 %copy-start.2 = (bf16[512,512]{1,0:T(8,128)(2,1)S(1)}, bf16[512,512]{1,0:T(8,128)(2,1)}, u32[]{:S(2)}) copy-start(bf16[512,512]{1,0:T(8,128)(2,1)} %w_out.1) | copy-start | bytes 1572868
  16.3 6.6 %copy-start.6 = (f32[2,512]{1,0:T(2,128)S(1)}, f32[2,512]{1,0:T(2,128)}, u32[]{:S(2)}) copy-start(f32[2,512]{1,0:T(2,128)} %gain.3) | copy-start | bytes 12292
  19.6 13.1 %collective-permute-start.4 = (bf16[128,1280]{1,0:T(8,128)(2,1)S(1)}, bf16[128,1280]{1,0:T(8,128)(2,1)S(1)}, u32[]{:S(2)}, u32[]{:S(2)}) collective-permute-start(bf16[128,1280]{1,0:T(8,128)(2,1)S(1)} %pack.1), channel_id=1, source_target_pairs={{0,15},{1,2},{2,1},{3,4},{4,3},{5,6},{6,5},{7,8},{8,7},{9,10},{10,... | collective-permute-start | bytes 983048 | tf_op jit(solution)/shard_map/ppermute | solution.py:317
  24.9 7.7 %copy-start = (bf16[2,512,512]{2,1,0:T(8,128)(2,1)S(1)}, bf16[2,512,512]{2,1,0:T(8,128)(2,1)}, u32[]{:S(2)}) copy-start(bf16[2,512,512]{2,1,0:T(8,128)(2,1)} %n_self.5) | copy-start | bytes 3145732
  25.0 9.9 %copy-start.3 = (bf16[2,512,512]{2,1,0:T(8,128)(2,1)S(1)}, bf16[2,512,512]{2,1,0:T(8,128)(2,1)}, u32[]{:S(2)}) copy-start(bf16[2,512,512]{2,1,0:T(8,128)(2,1)} %n_msg.3) | copy-start | bytes 3145732
  25.0 9.9 %copy-start.4 = (bf16[2,512,512]{2,1,0:T(8,128)(2,1)S(1)}, bf16[2,512,512]{2,1,0:T(8,128)(2,1)}, u32[]{:S(2)}) copy-start(bf16[2,512,512]{2,1,0:T(8,128)(2,1)} %n_out.3) | copy-start | bytes 3145732
  25.0 2.2 %collective-permute-start.2 = (bf16[128,512]{1,0:T(8,128)(2,1)S(1)}, bf16[128,512]{1,0:T(8,128)(2,1)S(1)}, u32[]{:S(2)}, u32[]{:S(2)}) collective-permute-start(bf16[128,512]{1,0:T(8,128)(2,1)S(1)} %get-tuple-element.31), channel_id=1, source_target_pairs={{0,1},{1,0},{2,3},{3,2},{4,5},{5,4},{6,7},{7,6},{8,9},{9,8},{10,11... | collective-permute-start | bytes 393224 | tf_op jit(solution)/shard_map/ppermute | solution.py:320
  27.5 10.2 %collective-permute-start.3 = (bf16[128,512]{1,0:T(8,128)(2,1)S(1)}, bf16[128,512]{1,0:T(8,128)(2,1)S(1)}, u32[]{:S(2)}, u32[]{:S(2)}) collective-permute-start(bf16[128,512]{1,0:T(8,128)(2,1)S(1)} %rim_message.1._), channel_id=1, source_target_pairs={{0,15},{1,2},{2,1},{3,4},{4,3},{5,6},{6,5},{7,8},{8,7},{9,10},{10,... | collective-permute-start | bytes 393224 | tf_op jit(solution)/shard_map/ppermute | solution.py:317
  36.9 1.4 %collective-permute-start.5 = (bf16[128,512]{1,0:T(8,128)(2,1)S(1)}, bf16[128,512]{1,0:T(8,128)(2,1)S(1)}, u32[]{:S(2)}, u32[]{:S(2)}) collective-permute-start(bf16[128,512]{1,0:T(8,128)(2,1)S(1)} %get-tuple-element.35), channel_id=1, source_target_pairs={{0,1},{1,0},{2,3},{3,2},{4,5},{5,4},{6,7},{7,6},{8,9},{9,8},{10,11... | collective-permute-start | bytes 393224 | tf_op jit(solution)/shard_map/ppermute | solution.py:320

commit v3 on v2

--- a/solution.py
+++ b/solution.py
@@ -44,92 +44,68 @@
 
 def pair_kernel(sides, cnt, tgt_hbm, src_hbm, obs, cpl, *refs):
     outs = refs[: len(sides)]
-    tgt, src, isem, xbuf, cbuf, acc, xsem, csem = refs[-8:]
-    blocks = outs[0].shape[0]
+    tgt, src, listed, xbuf, cbuf, acc, isem, csem, xsem = refs[-9:]
+    blocks, slots = outs[0].shape[0], xbuf.shape[0]
     odd = odd_device()
     parts = [{"off": 2 * odd, "on": 2 - 2 * odd, "self": 1}[side] for side in sides]
     reads = [
-        pltpu.make_async_copy(a, b, isem.at[i])
-        for i, (a, b) in enumerate(((tgt_hbm, tgt), (src_hbm, src)))
+        pltpu.make_async_copy(tgt_hbm, tgt, isem.at[0]),
+        pltpu.make_async_copy(src_hbm, src, isem.at[1]),
+        pltpu.make_async_copy(cpl, cbuf, csem),
     ]
     for read in reads:
         read.start()
-    for read in reads:
-        read.wait()
-    live = cnt[0]
-
-    def group(e):
+    reads[0].wait()
+    reads[1].wait()
+    groups = len(sides) * blocks
+
+    def fetch(e, words):
         t = tgt[e]
-        mine, place = jnp.bool_(False), jnp.int32(0)
+        mine, group = jnp.bool_(False), jnp.int32(0)
         for i, part in enumerate(parts):
             here = (t >= part * blocks) & (t < (part + 1) * blocks)
             mine = mine | here
-            place = jnp.where(here, t - part * blocks + i * blocks, place)
-        return place, mine
-
-    groups = len(sides) * blocks
-
-    def bump(words, place, mine):
+            group = jnp.where(here, t - part * blocks + i * blocks, group)
+        word = words[0]
+        for i in range(1, len(words)):
+            word = jnp.where(group >= 4 * i, words[i], word)
+        shift = 8 * (group & 3)
+
+        @pl.when(mine)
+        def _():
+            pltpu.make_async_copy(obs.at[src[e]], xbuf.at[e], xsem.at[e]).start()
+            listed[group * slots + ((word >> shift) & 255)] = e
+
         return [
-            word + jnp.where(mine & (place // 4 == i), 1 << (8 * (place % 4)), 0)
+            word + jnp.where(mine & (group >= 4 * i) & (group < 4 * i + 4), 1 << shift, 0)
             for i, word in enumerate(words)
         ]
 
-    def count(e, words):
-        return bump(words, *group(e))
-
-    words = lax.fori_loop(0, live, count, [jnp.int32(0)] * (groups // 4))
-    counts = [(words[g // 4] >> (8 * (g % 4))) & 255 for g in range(groups)]
-    firsts, total = [], jnp.int32(0)
+    words = lax.fori_loop(0, cnt[0], fetch, [jnp.int32(0)] * (groups // 4))
+    reads[2].wait()
+
     for g in range(groups):
-        firsts.append(total)
-        total = total + counts[g]
-    free = []
-    for i in range(groups // 4):
-        word = jnp.int32(0)
-        for j in range(4):
-            word = word + (firsts[4 * i + j] << (8 * j))
-        free.append(word)
-
-    def fetch(e, words):
-        place, mine = group(e)
-        word = words[0]
-        for i in range(1, len(words)):
-            word = jnp.where(place // 4 == i, words[i], word)
-
-        @pl.when(mine)
-        def _():
-            slot = (word >> (8 * (place % 4))) & 255
-            pltpu.make_async_copy(obs.at[src[e]], xbuf.at[slot], xsem.at[slot]).start()
-            pltpu.make_async_copy(cpl.at[e], cbuf.at[slot], csem.at[slot]).start()
-
-        return bump(words, place, mine)
-
-    lax.fori_loop(0, live, fetch, free)
-
-    def arrive(slot):
-        pltpu.make_async_copy(obs.at[0], xbuf.at[slot], xsem.at[slot]).wait()
-        pltpu.make_async_copy(cpl.at[0], cbuf.at[slot], csem.at[slot]).wait()
-
-    for g in range(groups):
+        number = (words[g // 4] >> (8 * (g % 4))) & 255
         acc[...] = jnp.zeros_like(acc)
 
-        def two(j, carry):
-            slot = firsts[g] + 2 * j
-            arrive(slot)
-            arrive(slot + 1)
-            left = jnp.concatenate([cbuf[slot], cbuf[slot + 1]], axis=1)
-            right = jnp.concatenate([xbuf[slot], xbuf[slot + 1]], axis=0)
+        def some(first, n):
+            at = [listed[g * slots + first + i] for i in range(n)]
+            for e in at:
+                pltpu.make_async_copy(obs.at[0], xbuf.at[e], xsem.at[e]).wait()
+            left = jnp.concatenate([cbuf[e] for e in at], axis=1)
+            right = jnp.concatenate([xbuf[e] for e in at], axis=0)
             acc[...] += dot(left, right)
+
+        def four(j, carry):
+            some(4 * j, 4)
             return carry
 
-        lax.fori_loop(0, counts[g] // 2, two, 0)
-
-        @pl.when(counts[g] % 2 == 1)
-        def _():
-            slot = firsts[g] + counts[g] - 1
-            arrive(slot)
-            acc[...] += dot(cbuf[slot], xbuf[slot])
+        lax.fori_loop(0, number // 4, four, 0)
+        for n in range(1, 4):
+
+            @pl.when(number % 4 == n)
+            def _():
+                some(number - n, n)
 
         out = outs[g // blocks]
         out[g % blocks] = acc[...].astype(out.dtype)
@@ -146,15 +122,16 @@
         scratch_shapes=[
             pltpu.SMEM((slots,), jnp.int32),
             pltpu.SMEM((slots,), jnp.int32),
-            pltpu.SemaphoreType.DMA((2,)),
+            pltpu.SMEM((len(sides) * blocks * slots,), jnp.int32),
             pltpu.VMEM((slots, rows, width), BF16),
             pltpu.VMEM((slots, rows, rows), BF16),
             pltpu.VMEM((rows, width), F32),
-            pltpu.SemaphoreType.DMA((slots,)),
+            pltpu.SemaphoreType.DMA((2,)),
+            pltpu.SemaphoreType.DMA,
             pltpu.SemaphoreType.DMA((slots,)),
         ],
         compiler_params=pltpu.CompilerParams(vmem_limit_bytes=12 << 20),
-        cost_estimate=pl.CostEstimate(flops=1 << 20, bytes_accessed=1 << 30, transcendentals=0),
+        cost_estimate=pl.CostEstimate(flops=1 << 20, bytes_accessed=1 << 20, transcendentals=0),
         name="pairs_" + "_".join(sides),
     )(cnt, *[pltpu.with_memory_space_constraint(x, pltpu.HBM) for x in (tgt, src, obs, cpl)], *more)
 
@@ -166,7 +143,7 @@
         in_specs=[SMEM] * len(scalars) + [VMEM] * len(arrays),
         out_specs=[VMEM] * len(out),
         compiler_params=pltpu.CompilerParams(vmem_limit_bytes=14 << 20),
-        cost_estimate=pl.CostEstimate(flops=1 << weight, bytes_accessed=1 << 24, transcendentals=0),
+        cost_estimate=pl.CostEstimate(flops=1 << weight, bytes_accessed=1 << 20, transcendentals=0),
         name=name,
     )(*scalars, *arrays)
 
@@ -195,19 +172,8 @@
             mix[cut, c * rows : (c + 1) * rows] = total.astype(BF16)
 
 
-def pack_kernel(rim, state_p, own, on, mix, packed):
-    rows, width = own.shape[1], own.shape[2]
-    size = state_p.shape[0]
-    m = block_order(rim)[0]
-    packed[:, :width] = state_p[:rows, :]
-    packed[:, width : 2 * width] = (own[m] + on[m].astype(F32)).astype(BF16)
-    packed[:, 2 * width : 2 * width + rows] = mix[:rows, size : size + rows]
-    lane = lax.broadcasted_iota(jnp.int32, (rows, 128), 1)
-    packed[:, 2 * width + rows :] = jnp.where(lane == m, 1.0, 0.0).astype(BF16)
-
-
-def encode_kernel(half, rim, pre, state_p, own, on, off, w_obs, w_out, gain, state, normed, *rims):
-    rows = own.shape[1]
+def encode_kernel(half, rim, pre, state_p, own, on, off, w_obs, w_out, gain, mix, state, normed, *rims):
+    blocks, rows = own.shape[0], own.shape[1]
     summed = jnp.concatenate(
         [
             (own[m] + on[m].astype(F32) + off[m].astype(F32)).astype(BF16)
@@ -221,7 +187,10 @@
     result = norm_rows(updated.astype(F32), gain[:1, :])
     normed[...] = result
     if rims:
+        width, size = state.shape[1], blocks * rows
         rims[0][...] = result[rows:, :]
+        rims[1][:, :width] = updated[:rows, :]
+        rims[1][:, width:] = mix[:rows, size : size + rows]
 
 
 def partial_kernel(mix, first, second, on, message):
@@ -233,20 +202,14 @@
     ).astype(BF16)
 
 
-def neighbour_kernel(packed, sent, first, gain, w_self, w_obs, w_out, node_gain, n_self, _, state, normed, pre, message):
+def neighbour_kernel(packed, first, node_gain, n_self, _, state, normed, pre, message):
     rows, width = state.shape
-    own = packed[:, :width]
-    summed = packed[:, width : 2 * width].astype(F32)
-    for t in range(sent.shape[0]):
-        mask = packed[:, 2 * width + rows + t : 2 * width + rows + t + 1].astype(F32)
-        summed = summed + mask * sent[t].astype(F32)
-    start = dot(norm_rows(own.astype(F32), gain[...]), w_self[...])
-    updated = update(own, start, summed.astype(BF16), w_obs[...], w_out[...])
-    state[...] = updated
-    result = norm_rows(updated.astype(F32), node_gain[:1, :])
+    values = packed[:, :width]
+    state[...] = values
+    result = norm_rows(values.astype(F32), node_gain[:1, :])
     normed[...] = result
     pre[...] = dot(result, n_self[0])
-    message[...] = dot(packed[:, 2 * width : 2 * width + rows], first[:rows, :])
+    message[...] = dot(packed[:, width:], first[:rows, :])
 
 
 def round_kernel(mix, first, second, off, on, state_a, state_b, n_self, n_msg, n_out, gain, state, normed, rim):
@@ -334,25 +297,18 @@
         [rim_send, neighbor],
         [mesh_state, enc_gain, enc_self, mesh_coupling],
         "prepare",
-        weight=40,
-    )
-    (packed,) = call(
-        pack_kernel,
-        [jax.ShapeDtypeStruct((rows, 2 * width + 2 * rows), BF16)],
-        [rim_send],
-        [state_p, sums_own, sums_on, mix],
-        "pack",
-    )
-    packed = swap_off(packed)
-    encode = (pre, state_p, sums_own, sums_on, sums_off, enc_obs, enc_out, node_gain)
-    state_a, first, rim_on = call(
+        weight=34,
+    )
+    encode = (pre, state_p, sums_own, sums_on, sums_off, enc_obs, enc_out, node_gain, mix)
+    state_a, first, rim_on, packed = call(
         lambda *refs: encode_kernel(0, *refs),
-        [wide(2 * rows), wide(2 * rows), wide(rows)],
+        [wide(2 * rows), wide(2 * rows), wide(rows), jax.ShapeDtypeStruct((rows, width + rows), BF16)],
         [rim_send],
         encode,
         "encode_rims",
     )
     on = swap_on(rim_on)
+    packed = swap_off(packed)
     state_b, second = call(
         lambda *refs: encode_kernel(1, *refs),
         [wide(2 * rows), wide(2 * rows)],
@@ -366,7 +322,7 @@
         neighbour_kernel,
         [wide(rows), wide(rows), wide(rows, F32), wide(rows, F32)],
         [],
-        [packed, sent, first, enc_gain, enc_self, enc_obs, enc_out, node_gain, node_self, message],
+        [packed, first, node_gain, node_self, message],
         "neighbour_rim",
     )
     state, normed, rim_on = call(

time: 40.9 us -> 35.4 us (0.87)
  the two profiles are of different devices: /device:TPU:0 before, /device:TPU:3 now
where the time goes in v3:
time: 35.4 us
  Pallas kernels  17.6 us (50%)
  starting transfers between devices  8.83 us (25%)
  waiting for transfers between devices  8.06 us (23%)
  between operations  0.86 us (2%)
    pallas_call x8, Pallas kernels, call(): pl.pallas_call(kernel, out_shape=out, in_specs=[SMEM] * len(scalars) + [V...  11.1 us
    ppermute x3, waiting for transfers between devices, swap_off(): return lax.ppermute(x, 'mesh', off_route)  7.79 us
    ppermute x3, starting transfers between devices, swap_on(): return lax.ppermute(x, 'mesh', on_route)  7.05 us
    pallas_call x2, Pallas kernels, pair_sums(): pl.pallas_call(lambda *refs: pair_kernel(list(sides), *refs[:5], *refs[5...  6.54 us
    ppermute x3, starting transfers between devices, swap_off(): return lax.ppermute(x, 'mesh', off_route)  1.78 us
  transfers between devices with their start and end apart: 6, of which 3 were waited for; matrix products, arithmetic and copies ran while one was open for 0% of the time, Pallas kernels for 28%

profile of v3, /device:TPU:3, one launch (start us, length us, event | category | flops | bytes accessed | tf_op | source)
XLA Modules:
  0.0 35.4 jit_solution(2796788848709005183)
XLA Ops:
  0.7 3.1 %pairs_off.1.refs_5_ = bf16[4,128,512]{2,1,0:T(8,128)(2,1)S(1)} custom-call(s32[1]{0:T(128)S(6)} %copy.18.refs_0_, s32[32]{0:T(128)} %refs_1_.3, s32[32]{0:T(128)} %refs_2_.3, bf16[32,128,512]{2,1,0:T(8,128)(2,1)} %refs_3_.3, bf16[32,128,128]{2,1,0:T(8,128)(2,1)} %refs_4_.3), custom_call_target="tpu_custom_call" | custom-call | flops 1048576 | bytes 1048576 | tf_op jit(solution)/shard_map/pairs_off/pallas_call | solution.py:117
  3.8 0.0 copy-start.6
  3.8 0.0 copy-start.7
  3.8 0.0 copy-start.8
  3.8 0.0 copy-start.9
  3.9 0.0 copy-start.10
  3.9 0.0 copy-start.11
  3.9 0.4 %collective-permute-start.1 = (bf16[4,128,512]{2,1,0:T(8,128)(2,1)S(1)}, bf16[4,128,512]{2,1,0:T(8,128)(2,1)S(1)}, u32[]{:S(2)}, u32[]{:S(2)}) collective-permute-start(bf16[4,128,512]{2,1,0:T(8,128)(2,1)S(1)} %pairs_off.1.refs_5_), channel_id=1, source_target_pairs={{0,15},{1,2},{2,1},{3,4},{4,3},{5,6},{6,5},{7,8},{8,7},{9,10},{10,... | collective-permute-start | bytes 1572872 | tf_op jit(solution)/shard_map/ppermute | solution.py:280
  4.3 3.4 %pairs_on_self.1 = (bf16[4,128,512]{2,1,0:T(8,128)(2,1)S(1)}, f32[4,128,512]{2,1,0:T(8,128)S(1)}) custom-call(s32[1]{0:T(128)S(6)} %copy.18.refs_0_, s32[32]{0:T(128)} %refs_1_.3, s32[32]{0:T(128)} %refs_2_.3, bf16[32,128,512]{2,1,0:T(8,128)(2,1)} %refs_3_.3, bf16[32,128,128]{2,1,0:T(8,128)(2,1)} %refs_4_.3, bf16[4,128,512]{2,1,0:T(8,128)(2,1)S(1)} %pairs_off.1.refs_5_), custom_call_target="tpu_custom_call" | custom-call | flops 1048576 | bytes 1048576 | tf_op jit(solution)/shard_map/pairs_on_self/pallas_call | solution.py:117
  7.7 2.8 %collective-permute-start = (bf16[4,128,512]{2,1,0:T(8,128)(2,1)S(1)}, bf16[4,128,512]{2,1,0:T(8,128)(2,1)S(1)}, u32[]{:S(2)}, u32[]{:S(2)}) collective-permute-start(bf16[4,128,512]{2,1,0:T(8,128)(2,1)S(1)} %get-tuple-element.29), channel_id=1, source_target_pairs={{0,1},{1,0},{2,3},{3,2},{4,5},{5,4},{6,7},{7,6},{8,9},{9,8},{10,11... | collective-permute-start | bytes 1572872 | tf_op jit(solution)/shard_map/ppermute | solution.py:283
  10.5 0.0 copy-start.3
  10.5 0.0 copy-start.4
  10.5 0.0 copy-start.5
  10.6 1.9 %prepare.1 = (f32[512,512]{1,0:T(8,128)S(1)}, bf16[512,512]{1,0:T(8,128)(2,1)S(1)}, bf16[512,768]{1,0:T(8,128)(2,1)S(1)}) custom-call(s32[1,2]{1,0:T(1,128)S(1)} %copy-done.6, s32[4,4]{1,0:T(4,128)S(1)} %copy-done.10, bf16[4,128,512]{2,1,0:T(8,128)(2,1)S(1)} %copy-done.7, f32[1,512]{1,0:T(1,128)S(1)} %bitcast.1, bf16[512,512]{1,0:T(8,128)(2,1)S(1)} %copy-done.8, ...), custom_call_target="tpu_custom_call" | custom-call | flops 17179869184 | bytes 1048576 | tf_op jit(solution)/shard_map/prepare/pallas_call | solution.py:140
  12.5 5.7 %collective-permute-done.1.refs_5_ = bf16[4,128,512]{2,1,0:T(8,128)(2,1)S(1)} collective-permute-done((bf16[4,128,512]{2,1,0:T(8,128)(2,1)S(1)}, bf16[4,128,512]{2,1,0:T(8,128)(2,1)S(1)}, u32[]{:S(2)}, u32[]{:S(2)}) %collective-permute-start.1) | collective-permute-done | bytes 524320 | tf_op jit(solution)/shard_map/ppermute | solution.py:280
  18.2 0.0 collective-permute-done.refs_4_
  18.2 1.3 %encode_rims.1 = (bf16[256,512]{1,0:T(8,128)(2,1)S(1)}, bf16[256,512]{1,0:T(8,128)(2,1)S(1)}, bf16[128,512]{1,0:T(8,128)(2,1)S(1)}, bf16[128,640]{1,0:T(8,128)(2,1)S(1)}) custom-call(s32[1,2]{1,0:T(1,128)S(1)} %copy-done.6, f32[512,512]{1,0:T(8,128)S(1)} %get-tuple-element.26.refs_1_, bf16[512,512]{1,0:T(8,128)(2,1)S(1)} %get-tuple-element.27.refs_2_, ...), custom_call_target="tpu_custom_call" | custom-call | flops 1048576 | bytes 1048576 | tf_op jit(solution)/shard_map/encode_rims/pallas_call | solution.py:140
  19.5 0.0 copy-start
  19.5 0.4 %collective-permute-start.4 = (bf16[128,640]{1,0:T(8,128)(2,1)S(1)}, bf16[128,640]{1,0:T(8,128)(2,1)S(1)}, u32[]{:S(2)}, u32[]{:S(2)}) collective-permute-start(bf16[128,640]{1,0:T(8,128)(2,1)S(1)} %get-tuple-element.33), channel_id=1, source_target_pairs={{0,15},{1,2},{2,1},{3,4},{4,3},{5,6},{6,5},{7,8},{8,7},{9,10},{10,... | collective-permute-start | bytes 491528 | tf_op jit(solution)/shard_map/ppermute | solution.py:280
  20.0 0.6 %collective-permute-start.2 = (bf16[128,512]{1,0:T(8,128)(2,1)S(1)}, bf16[128,512]{1,0:T(8,128)(2,1)S(1)}, u32[]{:S(2)}, u32[]{:S(2)}) collective-permute-start(bf16[128,512]{1,0:T(8,128)(2,1)S(1)} %get-tuple-element.32), channel_id=1, source_target_pairs={{0,1},{1,0},{2,3},{3,2},{4,5},{5,4},{6,7},{7,6},{8,9},{9,8},{10,11... | collective-permute-start | bytes 393224 | tf_op jit(solution)/shard_map/ppermute | solution.py:283
  20.5 1.3 %encode_others.1 = (bf16[256,512]{1,0:T(8,128)(2,1)S(1)}, bf16[256,512]{1,0:T(8,128)(2,1)S(1)}) custom-call(s32[1,2]{1,0:T(1,128)S(1)} %copy-done.6, f32[512,512]{1,0:T(8,128)S(1)} %get-tuple-element.26.refs_1_, bf16[512,512]{1,0:T(8,128)(2,1)S(1)} %get-tuple-element.27.refs_2_, f32[4,128,512]{2,1,0:T(8,128)S(1)} %get-tuple-element.28.refs_3_, ...), custom_call_target="tpu_custom_call" | custom-call | flops 1048576 | bytes 1048576 | tf_op jit(solution)/shard_map/encode_others/pallas_call | solution.py:140
  21.8 0.0 collective-permute-done.2.on
  21.8 0.3 rim_message.1._
  22.1 0.9 %collective-permute-start.3 = (bf16[128,512]{1,0:T(8,128)(2,1)S(1)}, bf16[128,512]{1,0:T(8,128)(2,1)S(1)}, u32[]{:S(2)}, u32[]{:S(2)}) collective-permute-start(bf16[128,512]{1,0:T(8,128)(2,1)S(1)} %rim_message.1._), channel_id=1, source_target_pairs={{0,15},{1,2},{2,1},{3,4},{4,3},{5,6},{6,5},{7,8},{8,7},{9,10},{10,... | collective-permute-start | bytes 393224 | tf_op jit(solution)/shard_map/ppermute | solution.py:280
  23.0 2.1 %collective-permute-done.4.packed = bf16[128,640]{1,0:T(8,128)(2,1)S(1)} collective-permute-done((bf16[128,640]{1,0:T(8,128)(2,1)S(1)}, bf16[128,640]{1,0:T(8,128)(2,1)S(1)}, u32[]{:S(2)}, u32[]{:S(2)}) %collective-permute-start.4) | collective-permute-done | bytes 163872 | tf_op jit(solution)/shard_map/ppermute | solution.py:280
  25.1 0.4 %neighbour_rim.1 = (bf16[128,512]{1,0:T(8,128)(2,1)S(1)}, bf16[128,512]{1,0:T(8,128)(2,1)S(1)}, f32[128,512]{1,0:T(8,128)S(1)}, f32[128,512]{1,0:T(8,128)S(1)}) custom-call(bf16[128,640]{1,0:T(8,128)(2,1)S(1)} %collective-permute-done.4.packed, bf16[256,512]{1,0:T(8,128)(2,1)S(1)} %get-tuple-element.30.first, f32[2,512]{1,0:T(2,128)S(1)} %copy-done.5, ...), custom_call_target="tpu_custom_call" | custom-call | flops 1048576 | bytes 1048576 | tf_op jit(solution)/shard_map/neighbour_rim/pallas_call | solution.py:140
  25.6 2.0 %round_0.1 = (bf16[512,512]{1,0:T(8,128)(2,1)S(1)}, bf16[512,512]{1,0:T(8,128)(2,1)S(1)}, bf16[128,512]{1,0:T(8,128)(2,1)S(1)}) custom-call(bf16[512,768]{1,0:T(8,128)(2,1)S(1)} %get-tuple-element.25.refs_9_.mix, bf16[256,512]{1,0:T(8,128)(2,1)S(1)} %get-tuple-element.30.first, bf16[256,512]{1,0:T(8,128)(2,1)S(1)} %get-tuple-element.31.second, ...), custom_call_target="tpu_custom_call" | custom-call | flops 1048576 | bytes 1048576 | tf_op jit(solution)/shard_map/round_0/pallas_call | solution.py:140
  27.5 3.7 %collective-permute-start.5 = (bf16[128,512]{1,0:T(8,128)(2,1)S(1)}, bf16[128,512]{1,0:T(8,128)(2,1)S(1)}, u32[]{:S(2)}, u32[]{:S(2)}) collective-permute-start(bf16[128,512]{1,0:T(8,128)(2,1)S(1)} %get-tuple-element.37), channel_id=1, source_target_pairs={{0,1},{1,0},{2,3},{3,2},{4,5},{5,4},{6,7},{7,6},{8,9},{9,8},{10,11... | collective-permute-start | bytes 393224 | tf_op jit(solution)/shard_map/ppermute | solution.py:283
  31.3 0.7 %round_1_local.1 = (f32[512,512]{1,0:T(8,128)S(1)}, f32[512,512]{1,0:T(8,128)S(1)}) custom-call(bf16[512,768]{1,0:T(8,128)(2,1)S(1)} %get-tuple-element.25.refs_9_.mix, bf16[512,512]{1,0:T(8,128)(2,1)S(1)} %get-tuple-element.41.normed, bf16[2,512,512]{2,1,0:T(8,128)(2,1)S(1)} %copy-done), custom_call_target="tpu_custom_call" | custom-call | flops 1048576 | bytes 1048576 | tf_op jit(solution)/shard_map/round_1_local/pallas_call | solution.py:140
  32.0 0.0 collective-permute-done.3.arrived
  32.0 0.3 collective-permute-done.5.on
  32.3 3.2 %round_1.1 = bf16[4,128,512]{2,1,0:T(8,128)(2,1)} custom-call(s32[1,2]{1,0:T(1,128)S(1)} %copy-done.6, bf16[128,512]{1,0:T(8,128)(2,1)S(1)} %collective-permute-done.3.arrived, bf16[128,512]{1,0:T(8,128)(2,1)S(1)} %collective-permute-done.5.on, f32[128,512]{1,0:T(8,128)S(1)} %get-tuple-element.38.far_message, f32[128,512]{1,0:T(8,128)S(1)} %get-tuple-element.39.far_pre, ...), custom_call_target="tpu_custom_call" | custom-call | flops 1048576 | bytes 1048576 | tf_op jit(solution)/shard_map/round_1/pallas_call | solution.py:140
  (14 shorter events, 0.0 us)
Async XLA Ops:
  3.8 6.7 %copy-start.6 = (s32[1,2]{1,0:T(1,128)S(1)}, s32[1,2]{1,0:T(1,128)}, u32[]{:S(2)}) copy-start(s32[1,2]{1,0:T(1,128)} %rim.3) | copy-start | bytes 28
  3.8 6.7 %copy-start.7 = (bf16[4,128,512]{2,1,0:T(8,128)(2,1)S(1)}, bf16[4,128,512]{2,1,0:T(8,128)(2,1)}, u32[]{:S(2)}) copy-start(bf16[4,128,512]{2,1,0:T(8,128)(2,1)} %state.1) | copy-start | bytes 1572868
  3.8 6.7 %copy-start.8 = (bf16[512,512]{1,0:T(8,128)(2,1)S(1)}, bf16[512,512]{1,0:T(8,128)(2,1)}, u32[]{:S(2)}) copy-start(bf16[512,512]{1,0:T(8,128)(2,1)} %w_self.1) | copy-start | bytes 1572868
  3.8 6.6 %copy-start.9 = (bf16[4,4,128,128]{3,2,1,0:T(8,128)(2,1)S(1)}, bf16[4,4,128,128]{3,2,1,0:T(8,128)(2,1)}, u32[]{:S(2)}) copy-start(bf16[4,4,128,128]{3,2,1,0:T(8,128)(2,1)} %coupling.1) | copy-start | bytes 1572868
  3.9 6.6 %copy-start.10 = (s32[4,4]{1,0:T(4,128)S(1)}, s32[4,4]{1,0:T(4,128)}, u32[]{:S(2)}) copy-start(s32[4,4]{1,0:T(4,128)} %nbr.1) | copy-start | bytes 196
  3.9 6.6 %copy-start.11 = (f32[512]{0:T(512)S(1)}, f32[512]{0:T(512)}, u32[]{:S(2)}) copy-start(f32[512]{0:T(512)} %param.26) | copy-start | bytes 6148
  3.9 14.3 %collective-permute-start.1 = (bf16[4,128,512]{2,1,0:T(8,128)(2,1)S(1)}, bf16[4,128,512]{2,1,0:T(8,128)(2,1)S(1)}, u32[]{:S(2)}, u32[]{:S(2)}) collective-permute-start(bf16[4,128,512]{2,1,0:T(8,128)(2,1)S(1)} %pairs_off.1.refs_5_), channel_id=1, source_target_pairs={{0,15},{1,2},{2,1},{3,4},{4,3},{5,6},{6,5},{7,8},{8,7},{9,10},{10,... | collective-permute-start | bytes 1572872 | tf_op jit(solution)/shard_map/ppermute | solution.py:280
  7.7 10.5 %collective-permute-start = (bf16[4,128,512]{2,1,0:T(8,128)(2,1)S(1)}, bf16[4,128,512]{2,1,0:T(8,128)(2,1)S(1)}, u32[]{:S(2)}, u32[]{:S(2)}) collective-permute-start(bf16[4,128,512]{2,1,0:T(8,128)(2,1)S(1)} %get-tuple-element.29), channel_id=1, source_target_pairs={{0,1},{1,0},{2,3},{3,2},{4,5},{5,4},{6,7},{7,6},{8,9},{9,8},{10,11... | collective-permute-start | bytes 1572872 | tf_op jit(solution)/shard_map/ppermute | solution.py:283
  10.5 7.7 %copy-start.3 = (bf16[512,512]{1,0:T(8,128)(2,1)S(1)}, bf16[512,512]{1,0:T(8,128)(2,1)}, u32[]{:S(2)}) copy-start(bf16[512,512]{1,0:T(8,128)(2,1)} %refs_6_.3) | copy-start | bytes 1572868
  10.5 7.7 %copy-start.4 = (bf16[512,512]{1,0:T(8,128)(2,1)S(1)}, bf16[512,512]{1,0:T(8,128)(2,1)}, u32[]{:S(2)}) copy-start(bf16[512,512]{1,0:T(8,128)(2,1)} %refs_7_.3) | copy-start | bytes 1572868
  10.5 7.6 %copy-start.5 = (f32[2,512]{1,0:T(2,128)S(1)}, f32[2,512]{1,0:T(2,128)}, u32[]{:S(2)}) copy-start(f32[2,512]{1,0:T(2,128)} %gain.3) | copy-start | bytes 12292
  19.5 5.6 %copy-start = (bf16[2,512,512]{2,1,0:T(8,128)(2,1)S(1)}, bf16[2,512,512]{2,1,0:T(8,128)(2,1)}, u32[]{:S(2)}) copy-start(bf16[2,512,512]{2,1,0:T(8,128)(2,1)} %n_self.5) | copy-start | bytes 3145732
  19.5 5.6 %collective-permute-start.4 = (bf16[128,640]{1,0:T(8,128)(2,1)S(1)}, bf16[128,640]{1,0:T(8,128)(2,1)S(1)}, u32[]{:S(2)}, u32[]{:S(2)}) collective-permute-start(bf16[128,640]{1,0:T(8,128)(2,1)S(1)} %get-tuple-element.33), channel_id=1, source_target_pairs={{0,15},{1,2},{2,1},{3,4},{4,3},{5,6},{6,5},{7,8},{8,7},{9,10},{10,... | collective-permute-start | bytes 491528 | tf_op jit(solution)/shard_map/ppermute | solution.py:280
  20.0 5.6 %copy-start.1 = (bf16[2,512,512]{2,1,0:T(8,128)(2,1)S(1)}, bf16[2,512,512]{2,1,0:T(8,128)(2,1)}, u32[]{:S(2)}) copy-start(bf16[2,512,512]{2,1,0:T(8,128)(2,1)} %n_msg.3) | copy-start | bytes 3145732
  20.0 5.6 %copy-start.2 = (bf16[2,512,512]{2,1,0:T(8,128)(2,1)S(1)}, bf16[2,512,512]{2,1,0:T(8,128)(2,1)}, u32[]{:S(2)}) copy-start(bf16[2,512,512]{2,1,0:T(8,128)(2,1)} %n_out.3) | copy-start | bytes 3145732
  20.0 1.9 %collective-permute-start.2 = (bf16[128,512]{1,0:T(8,128)(2,1)S(1)}, bf16[128,512]{1,0:T(8,128)(2,1)S(1)}, u32[]{:S(2)}, u32[]{:S(2)}) collective-permute-start(bf16[128,512]{1,0:T(8,128)(2,1)S(1)} %get-tuple-element.32), channel_id=1, source_target_pairs={{0,1},{1,0},{2,3},{3,2},{4,5},{5,4},{6,7},{7,6},{8,9},{9,8},{10,11... | collective-permute-start | bytes 393224 | tf_op jit(solution)/shard_map/ppermute | solution.py:283
  22.1 9.9 %collective-permute-start.3 = (bf16[128,512]{1,0:T(8,128)(2,1)S(1)}, bf16[128,512]{1,0:T(8,128)(2,1)S(1)}, u32[]{:S(2)}, u32[]{:S(2)}) collective-permute-start(bf16[128,512]{1,0:T(8,128)(2,1)S(1)} %rim_message.1._), channel_id=1, source_target_pairs={{0,15},{1,2},{2,1},{3,4},{4,3},{5,6},{6,5},{7,8},{8,7},{9,10},{10,... | collective-permute-start | bytes 393224 | tf_op jit(solution)/shard_map/ppermute | solution.py:280
  27.5 4.7 %collective-permute-start.5 = (bf16[128,512]{1,0:T(8,128)(2,1)S(1)}, bf16[128,512]{1,0:T(8,128)(2,1)S(1)}, u32[]{:S(2)}, u32[]{:S(2)}) collective-permute-start(bf16[128,512]{1,0:T(8,128)(2,1)S(1)} %get-tuple-element.37), channel_id=1, source_target_pairs={{0,1},{1,0},{2,3},{3,2},{4,5},{5,4},{6,7},{7,6},{8,9},{9,8},{10,11... | collective-permute-start | bytes 393224 | tf_op jit(solution)/shard_map/ppermute | solution.py:283
